TPU v7x, 128 devices: a whole 4x4x4 slice. The times are simulated.
128 devices in a mesh: gx: 8 (over x, core), gy: 16 (over y, z).
Axes of the slice: x: 4, y: 4, z: 4, core: 2. Of those that a mesh axis runs over, the one named last changes fastest.
Arguments:
- pressure_source: float32 [192, 384, 384], P('gx', 'gy'), may hold values from -6 to 6
- building_heights: int32 [32, 64], replicated, may hold values from 0 to 63
Outputs:
- correction: float32 [192, 384, 384], P('gx', 'gy')
- coarse_solution: float32 [64, 128, 128], P('gx', 'gy')
Inputs may be any that keep to these rules, and one draw needn't show every extreme that they name: `building_heights`: the height of the building in each element column, in elements, so that the top layer of every column is fluid.
All inputs are finite; a program needn't handle non-finite values.
Results may differ from a plain program's by a relative error of at most 0.0003.
Values sent between devices are 32-bit elements; how exact they have to be, the bound alone decides.
No kernel may reach another device: no remote copies, remote signals or barrier semaphores. Data moves between devices by JAX's collectives and lax.ppermute only.
A program may use at most 128 MiB of HBM per device.

v0:
```python
import jax
import jax.numpy as jnp
import numpy as np
from jax import lax
from jax.sharding import PartitionSpec as P

CG_ITERS = 10


HIGHEST = lax.Precision.HIGHEST


def with_halo(cells, sides, width):
    for axis, dim in sides:
        count = lax.axis_size(axis)
        ends = count - 1
        head = lax.slice_in_dim(cells, 0, width, axis=dim)
        tail = lax.slice_in_dim(cells, cells.shape[dim] - width, cells.shape[dim], axis=dim)
        cells = jnp.concatenate(
            [
                lax.ppermute(tail, axis, [(i, (i + 1) % count) for i in range(ends)]),
                cells,
                lax.ppermute(head, axis, [((i + 1) % count, i) for i in range(ends)]),
            ],
            axis=dim,
        )
    return cells


def gll_nodes(node_count):
    if node_count == 6:
        outer_point = 0.7650553239294647
        inner_point = 0.2852315164806451
        points = [-1.0, -outer_point, -inner_point, inner_point, outer_point, 1.0]
        weights = [
            1.0 / 15.0,
            0.378474956297847,
            0.5548583770354863,
            0.5548583770354863,
            0.378474956297847,
            1.0 / 15.0,
        ]
    elif node_count == 4:
        inner_point = 0.4472135954999579
        points = [-1.0, -inner_point, inner_point, 1.0]
        weights = [1.0 / 6.0, 5.0 / 6.0, 5.0 / 6.0, 1.0 / 6.0]
    else:
        points = [-1.0, 1.0]
        weights = [1.0, 1.0]
    return (np.array(points), np.array(weights))


def diagonal_of(matrix):
    return np.array([matrix[index_id, index_id] for index_id in range(matrix.shape[0])])


def lagrange_tables(node_count):
    points, weights = gll_nodes(node_count)
    others = [
        [points[col_id] - points[other] for other in range(node_count) if other != col_id]
        for col_id in range(node_count)
    ]
    bary_weights = np.array([1.0 / np.prod(entries) for entries in others])
    derivative = np.zeros((node_count, node_count))
    for row_id in range(node_count):
        for col_id in range(node_count):
            if row_id != col_id:
                derivative[row_id, col_id] = (
                    bary_weights[col_id] / bary_weights[row_id] / (points[row_id] - points[col_id])
                )
        derivative[row_id, row_id] = -np.sum(derivative[row_id])
    stiffness = derivative.T @ (weights[:, None] * derivative)
    return (stiffness, weights)


def interpolation(coarse_count, fine_count):
    coarse_points = gll_nodes(coarse_count)[0]
    fine_points = gll_nodes(fine_count)[0]
    matrix = np.ones((fine_count, coarse_count))
    for row_id in range(fine_count):
        for col_id in range(coarse_count):
            for other in range(coarse_count):
                if other != col_id:
                    matrix[row_id, col_id] *= (fine_points[row_id] - coarse_points[other]) / (
                        coarse_points[col_id] - coarse_points[other]
                    )
    return matrix


def chebyshev_bounds(node_count):
    stiffness, weights = lagrange_tables(node_count)
    row_abs = np.abs(stiffness).sum(axis=1)
    diag_vals = diagonal_of(stiffness)
    wide_one = weights[:, None, None]
    wide_two = weights[None, :, None]
    wide_three = weights[None, None, :]
    numerator = (
        row_abs[:, None, None] * wide_two * wide_three
        + wide_one * row_abs[None, :, None] * wide_three
        + wide_one * wide_two * row_abs[None, None, :]
    )
    denominator = (
        diag_vals[:, None, None] * wide_two * wide_three
        + wide_one * diag_vals[None, :, None] * wide_three
        + wide_one * wide_two * diag_vals[None, None, :]
    )
    top_bound = float(np.max(numerator / denominator))
    return (top_bound, 0.1 * top_bound)


def tiled(vector, length, position):
    repeated = jnp.asarray(np.tile(vector, length // vector.shape[0]), jnp.float32)
    return repeated.reshape(tuple((length if axis_id == position else 1 for axis_id in range(3))))


def along_first(values, matrix):
    out_count, in_count = matrix.shape
    blocks = values.shape[0] // in_count
    shaped = values.reshape(blocks, in_count, values.shape[1] * values.shape[2])
    result = jnp.einsum("ip,xpr->xir", jnp.asarray(matrix, jnp.float32), shaped, precision=HIGHEST)
    return result.reshape(blocks * out_count, values.shape[1], values.shape[2])


def along_second(values, matrix):
    out_count, in_count = matrix.shape
    blocks = values.shape[1] // in_count
    shaped = values.reshape(values.shape[0], blocks, in_count, values.shape[2])
    result = jnp.einsum(
        "jq,xyqc->xyjc", jnp.asarray(matrix, jnp.float32), shaped, precision=HIGHEST
    )
    return result.reshape(values.shape[0], blocks * out_count, values.shape[2])


def along_third(values, matrix):
    out_count, in_count = matrix.shape
    blocks = values.shape[2] // in_count
    block_matrix = jnp.asarray(np.kron(np.eye(blocks), matrix.T), jnp.float32)
    result = jnp.dot(values.reshape(-1, values.shape[2]), block_matrix, precision=HIGHEST)
    return result.reshape(values.shape[0], values.shape[1], blocks * out_count)


def pass_first(padded, node_count):
    position = np.arange(padded.shape[0] - 2) % node_count
    at_start = jnp.asarray(position == 0, jnp.float32)[:, None, None]
    at_end = jnp.asarray(position == node_count - 1, jnp.float32)[:, None, None]
    return padded[1:-1] + at_start * padded[:-2] + at_end * padded[2:]


def pass_second(padded, node_count):
    position = np.arange(padded.shape[1] - 2) % node_count
    at_start = jnp.asarray(position == 0, jnp.float32)[None, :, None]
    at_end = jnp.asarray(position == node_count - 1, jnp.float32)[None, :, None]
    return padded[:, 1:-1] + at_start * padded[:, :-2] + at_end * padded[:, 2:]


def pass_third(values, node_count):
    position = np.arange(values.shape[2]) % node_count
    at_start = jnp.asarray(position == 0, jnp.float32)[None, None, :]
    at_end = jnp.asarray(position == node_count - 1, jnp.float32)[None, None, :]
    earlier = jnp.pad(values[:, :, :-1], ((0, 0), (0, 0), (1, 0)))
    following = jnp.pad(values[:, :, 1:], ((0, 0), (0, 0), (0, 1)))
    return values + at_start * earlier + at_end * following


def rim_joint(values):
    return with_halo(values, (("gx", 0), ("gy", 1)), 1)


def assemble(values, node_count):
    summed = pass_third(values, node_count)
    padded = rim_joint(summed)
    return pass_second(pass_first(padded, node_count), node_count)


def spread_counts(elem_pad, node_count):
    position = np.arange(node_count)
    at_start = jnp.asarray(position == 0, jnp.float32)
    at_end = jnp.asarray(position == node_count - 1, jnp.float32)
    step_one = (
        elem_pad[1:-1][:, None]
        + at_start[None, :, None, None] * elem_pad[:-2][:, None]
        + at_end[None, :, None, None] * elem_pad[2:][:, None]
    )
    step_one = step_one.reshape(-1, elem_pad.shape[1], elem_pad.shape[2])
    step_two = (
        step_one[:, 1:-1][:, :, None]
        + at_start[None, None, :, None] * step_one[:, :-2][:, :, None]
        + at_end[None, None, :, None] * step_one[:, 2:][:, :, None]
    )
    step_two = step_two.reshape(step_one.shape[0], -1, elem_pad.shape[2])
    step_three = (
        step_two[:, :, 1:-1][:, :, :, None]
        + at_start * step_two[:, :, :-2][:, :, :, None]
        + at_end * step_two[:, :, 2:][:, :, :, None]
    )
    return step_three.reshape(step_two.shape[0], step_two.shape[1], -1)


def level_data(fluid_pad, exist_pad, node_count):
    fluid_count = spread_counts(fluid_pad, node_count)
    exist_count = spread_counts(exist_pad, node_count)
    ground = jnp.asarray(np.arange(fluid_count.shape[2]) > 0, jnp.float32)[None, None, :]
    node_mask = (
        (fluid_count == exist_count).astype(jnp.float32)
        * (fluid_count > 0.5).astype(jnp.float32)
        * ground
    )
    node_weight = 1.0 / exist_count
    fluid_cells = fluid_pad[1:-1, 1:-1, 1:-1]
    fluid_node = jnp.repeat(
        jnp.repeat(jnp.repeat(fluid_cells, node_count, axis=0), node_count, axis=1),
        node_count,
        axis=2,
    )
    stiffness, weights = lagrange_tables(node_count)
    stiff_diag = diagonal_of(stiffness)
    dims_now = fluid_count.shape
    local_diag = (
        tiled(stiff_diag, dims_now[0], 0)
        * tiled(weights, dims_now[1], 1)
        * tiled(weights, dims_now[2], 2)
    )
    local_diag = local_diag + tiled(weights, dims_now[0], 0) * tiled(
        stiff_diag, dims_now[1], 1
    ) * tiled(weights, dims_now[2], 2)
    local_diag = local_diag + tiled(weights, dims_now[0], 0) * tiled(
        weights, dims_now[1], 1
    ) * tiled(stiff_diag, dims_now[2], 2)
    inverse_diag = node_mask / (fluid_count * local_diag + 1.0 - node_mask)
    return (node_count, fluid_node, node_mask, node_weight, inverse_diag)


def element_action(values, level_info):
    node_count, fluid_node = (level_info[0], level_info[1])
    stiffness, weights = lagrange_tables(node_count)
    mass_first = tiled(weights, values.shape[0], 0)
    mass_second = tiled(weights, values.shape[1], 1)
    mass_third = tiled(weights, values.shape[2], 2)
    summed_terms = mass_second * mass_third * along_first(values, stiffness)
    summed_terms = summed_terms + mass_first * mass_third * along_second(values, stiffness)
    summed_terms = summed_terms + mass_first * mass_second * along_third(values, stiffness)
    return fluid_node * summed_terms


def apply_operator(values, level_info, assembler):
    return level_info[2] * assembler(element_action(values, level_info), level_info[0])


def smooth(target, start, level_info, bounds, assembler, from_zero):
    top_bound, low_bound = bounds
    center = 0.5 * (top_bound + low_bound)
    half_width = 0.5 * (top_bound - low_bound)
    inverse_diag = level_info[4]
    if from_zero:
        residual_now = target
        update = inverse_diag * residual_now / center
        solution = update
    else:
        residual_now = target - apply_operator(start, level_info, assembler)
        update = inverse_diag * residual_now / center
        solution = start + update
    residual_now = residual_now - apply_operator(update, level_info, assembler)
    rho_first = half_width / center
    rho_next = 1.0 / (2.0 * center / half_width - rho_first)
    update = (
        rho_next * rho_first * update + 2.0 * rho_next / half_width * inverse_diag * residual_now
    )
    return solution + update


def restrict(values, coarse_count, fine_count):
    matrix = interpolation(coarse_count, fine_count).T
    return along_third(along_second(along_first(values, matrix), matrix), matrix)


def prolong(values, coarse_count, fine_count):
    matrix = interpolation(coarse_count, fine_count)
    return along_third(along_second(along_first(values, matrix), matrix), matrix)


def conjugate_gradients(target, level_info, assembler, reduce_sum):
    node_weight = level_info[3]
    norm_start = reduce_sum(jnp.sum(node_weight * target * target))

    def iterate(index, cg_state):
        solution, residual_now, direction, norm_now = cg_state
        applied = apply_operator(direction, level_info, assembler)
        step_len = norm_now / reduce_sum(jnp.sum(node_weight * direction * applied))
        solution = solution + step_len * direction
        residual_now = residual_now - step_len * applied
        norm_next = reduce_sum(jnp.sum(node_weight * residual_now * residual_now))
        direction = residual_now + norm_next / norm_now * direction
        return (solution, residual_now, direction, norm_next)

    final_state = lax.fori_loop(
        0, CG_ITERS, iterate, (jnp.zeros_like(target), target, target, norm_start)
    )
    return final_state[0]


def sum_spread(partial_sum):
    return lax.psum(partial_sum, ("gx", "gy"))


def coarse_spread(target, level_info):
    return conjugate_gradients(target, level_info, assemble, sum_spread)


def per_device(pressure_source, building_heights):
    side_first = pressure_source.shape[0] // 6
    side_second = pressure_source.shape[1] // 6
    column = pressure_source.shape[2] // 6
    start_first = lax.axis_index("gx") * side_first
    start_second = lax.axis_index("gy") * side_second
    heights_pad = jnp.pad(building_heights, 1, constant_values=column)
    local_heights = lax.dynamic_slice(
        heights_pad, (start_first, start_second), (side_first + 2, side_second + 2)
    )
    exist_cols = lax.dynamic_slice(
        jnp.pad(jnp.ones(building_heights.shape, jnp.float32), 1),
        (start_first, start_second),
        (side_first + 2, side_second + 2),
    )
    layers = jnp.arange(-1, column + 1, dtype=jnp.int32)
    inside = ((layers >= 0) & (layers < column)).astype(jnp.float32)[None, None, :]
    fluid_pad = (layers[None, None, :] >= local_heights[:, :, None]).astype(jnp.float32) * inside
    exist_pad = exist_cols[:, :, None] * inside
    fine_level = level_data(fluid_pad, exist_pad, 6)
    middle_level = level_data(fluid_pad, exist_pad, 4)
    coarse_level = level_data(fluid_pad, exist_pad, 2)
    fine_bounds = chebyshev_bounds(6)
    middle_bounds = chebyshev_bounds(4)
    target_fine = fine_level[2] * assemble(pressure_source, 6)
    fine_sol = smooth(target_fine, None, fine_level, fine_bounds, assemble, True)
    fine_res = target_fine - apply_operator(fine_sol, fine_level, assemble)
    target_middle = middle_level[2] * assemble(restrict(fine_level[3] * fine_res, 4, 6), 4)
    middle_sol = smooth(target_middle, None, middle_level, middle_bounds, assemble, True)
    middle_res = target_middle - apply_operator(middle_sol, middle_level, assemble)
    target_coarse = coarse_level[2] * assemble(restrict(middle_level[3] * middle_res, 2, 4), 2)
    coarse_sol = coarse_spread(target_coarse, coarse_level)
    middle_sol = middle_sol + middle_level[2] * prolong(coarse_sol, 2, 4)
    middle_sol = smooth(target_middle, middle_sol, middle_level, middle_bounds, assemble, False)
    fine_sol = fine_sol + fine_level[2] * prolong(middle_sol, 4, 6)
    fine_sol = smooth(target_fine, fine_sol, fine_level, fine_bounds, assemble, False)
    return (fine_sol, coarse_sol)


def solution(mesh):
    in_specs = (P("gx", "gy", None), P())
    out_specs = (P("gx", "gy", None), P("gx", "gy", None))
    return jax.shard_map(
        per_device, mesh=mesh, in_specs=in_specs, out_specs=out_specs, check_vma=False
    )
```

profile of v0, /device:TPU:1, one launch (start us, length us, event | category | flops | bytes accessed | tf_op | source)
XLA Modules:
  0.0 2164.7 jit_solution(11092381032411942674)
XLA Ops:
  2.9 4.5 collective-permute-start.4
  23.5 4.6 copy.272
  31.0 4.7 copy.273
  38.5 4.7 copy.275
  45.9 4.7 copy.281
  53.4 4.6 copy.282
  60.9 4.7 copy.284
  103.8 4.3 collective-permute-start.10
  167.2 6.3 collective-permute-start.18
  275.2 4.3 collective-permute-start.26
  324.6 71.3 %psum.27 = f32[]{:T(128)} all-reduce(f32[]{:T(128)} %get-tuple-element.560), channel_id=1, replica_groups=mesh['gx'=8,'gy'=16] {'gx','gy'}, use_global_device_ids=true, to_apply=%region_1.2 | all-reduce | flops 1 | bytes 8 | tf_op jit(solution)/shard_map/psum | solution.py:302
  395.9 1636.0 %while.23 = (s32[]{:T(128)}, f32[8,8,128]{2,1,0:T(8,128)}, f32[8,8,128]{2,1,0:T(8,128)}, f32[8,8,128]{2,1,0:T(8,128)S(1)}, f32[]{:T(128)}, /*index=5*/f32[8,8,64...) while((s32[]{:T(128)}, f32[8,8,128]{2,1,0:T(8,128)}, ...), condition=%wide.region_7.8_spmd.clone.clone.clone.clone.clone, body=%wide.region_2.7_spmd.sunk.clone.clone.clone.clone.clone.sunk | while | flops 13401093 | bytes 2653795 | solution.py:295
  426.7 65.6 %psum.42 = f32[]{:T(128)} all-reduce(f32[]{:T(128)} %get-tuple-element.823), channel_id=1, replica_groups=mesh['gx'=8,'gy'=16] {'gx','gy'}, use_global_device_ids=true, to_apply=%region_4.4 | all-reduce | flops 1 | bytes 8 | tf_op jit(solution)/shard_map/while/body/eval_jaxpr/psum | solution.py:302
  495.0 62.5 %psum.43 = f32[]{:T(128)} all-reduce(f32[]{:T(128)} %get-tuple-element.825), channel_id=1, replica_groups=mesh['gx'=8,'gy'=16] {'gx','gy'}, use_global_device_ids=true, to_apply=%region_6.6 | all-reduce | flops 1 | bytes 8 | tf_op jit(solution)/shard_map/while/body/eval_jaxpr/psum | solution.py:302
  590.2 65.7 %psum.42 = f32[]{:T(128)} all-reduce(f32[]{:T(128)} %get-tuple-element.823), channel_id=1, replica_groups=mesh['gx'=8,'gy'=16] {'gx','gy'}, use_global_device_ids=true, to_apply=%region_4.4 | all-reduce | flops 1 | bytes 8 | tf_op jit(solution)/shard_map/while/body/eval_jaxpr/psum | solution.py:302
  658.6 62.5 %psum.43 = f32[]{:T(128)} all-reduce(f32[]{:T(128)} %get-tuple-element.825), channel_id=1, replica_groups=mesh['gx'=8,'gy'=16] {'gx','gy'}, use_global_device_ids=true, to_apply=%region_6.6 | all-reduce | flops 1 | bytes 8 | tf_op jit(solution)/shard_map/while/body/eval_jaxpr/psum | solution.py:302
  754.0 65.5 %psum.42 = f32[]{:T(128)} all-reduce(f32[]{:T(128)} %get-tuple-element.823), channel_id=1, replica_groups=mesh['gx'=8,'gy'=16] {'gx','gy'}, use_global_device_ids=true, to_apply=%region_4.4 | all-reduce | flops 1 | bytes 8 | tf_op jit(solution)/shard_map/while/body/eval_jaxpr/psum | solution.py:302
  822.2 62.5 %psum.43 = f32[]{:T(128)} all-reduce(f32[]{:T(128)} %get-tuple-element.825), channel_id=1, replica_groups=mesh['gx'=8,'gy'=16] {'gx','gy'}, use_global_device_ids=true, to_apply=%region_6.6 | all-reduce | flops 1 | bytes 8 | tf_op jit(solution)/shard_map/while/body/eval_jaxpr/psum | solution.py:302
  917.5 65.5 %psum.42 = f32[]{:T(128)} all-reduce(f32[]{:T(128)} %get-tuple-element.823), channel_id=1, replica_groups=mesh['gx'=8,'gy'=16] {'gx','gy'}, use_global_device_ids=true, to_apply=%region_4.4 | all-reduce | flops 1 | bytes 8 | tf_op jit(solution)/shard_map/while/body/eval_jaxpr/psum | solution.py:302
  985.8 62.5 %psum.43 = f32[]{:T(128)} all-reduce(f32[]{:T(128)} %get-tuple-element.825), channel_id=1, replica_groups=mesh['gx'=8,'gy'=16] {'gx','gy'}, use_global_device_ids=true, to_apply=%region_6.6 | all-reduce | flops 1 | bytes 8 | tf_op jit(solution)/shard_map/while/body/eval_jaxpr/psum | solution.py:302
  1081.1 65.5 %psum.42 = f32[]{:T(128)} all-reduce(f32[]{:T(128)} %get-tuple-element.823), channel_id=1, replica_groups=mesh['gx'=8,'gy'=16] {'gx','gy'}, use_global_device_ids=true, to_apply=%region_4.4 | all-reduce | flops 1 | bytes 8 | tf_op jit(solution)/shard_map/while/body/eval_jaxpr/psum | solution.py:302
  1149.3 62.5 %psum.43 = f32[]{:T(128)} all-reduce(f32[]{:T(128)} %get-tuple-element.825), channel_id=1, replica_groups=mesh['gx'=8,'gy'=16] {'gx','gy'}, use_global_device_ids=true, to_apply=%region_6.6 | all-reduce | flops 1 | bytes 8 | tf_op jit(solution)/shard_map/while/body/eval_jaxpr/psum | solution.py:302
  1244.7 65.5 %psum.42 = f32[]{:T(128)} all-reduce(f32[]{:T(128)} %get-tuple-element.823), channel_id=1, replica_groups=mesh['gx'=8,'gy'=16] {'gx','gy'}, use_global_device_ids=true, to_apply=%region_4.4 | all-reduce | flops 1 | bytes 8 | tf_op jit(solution)/shard_map/while/body/eval_jaxpr/psum | solution.py:302
  1312.9 62.5 %psum.43 = f32[]{:T(128)} all-reduce(f32[]{:T(128)} %get-tuple-element.825), channel_id=1, replica_groups=mesh['gx'=8,'gy'=16] {'gx','gy'}, use_global_device_ids=true, to_apply=%region_6.6 | all-reduce | flops 1 | bytes 8 | tf_op jit(solution)/shard_map/while/body/eval_jaxpr/psum | solution.py:302
  1408.3 65.5 %psum.42 = f32[]{:T(128)} all-reduce(f32[]{:T(128)} %get-tuple-element.823), channel_id=1, replica_groups=mesh['gx'=8,'gy'=16] {'gx','gy'}, use_global_device_ids=true, to_apply=%region_4.4 | all-reduce | flops 1 | bytes 8 | tf_op jit(solution)/shard_map/while/body/eval_jaxpr/psum | solution.py:302
  1476.5 62.5 %psum.43 = f32[]{:T(128)} all-reduce(f32[]{:T(128)} %get-tuple-element.825), channel_id=1, replica_groups=mesh['gx'=8,'gy'=16] {'gx','gy'}, use_global_device_ids=true, to_apply=%region_6.6 | all-reduce | flops 1 | bytes 8 | tf_op jit(solution)/shard_map/while/body/eval_jaxpr/psum | solution.py:302
  1571.9 65.5 %psum.42 = f32[]{:T(128)} all-reduce(f32[]{:T(128)} %get-tuple-element.823), channel_id=1, replica_groups=mesh['gx'=8,'gy'=16] {'gx','gy'}, use_global_device_ids=true, to_apply=%region_4.4 | all-reduce | flops 1 | bytes 8 | tf_op jit(solution)/shard_map/while/body/eval_jaxpr/psum | solution.py:302
  1640.1 62.5 %psum.43 = f32[]{:T(128)} all-reduce(f32[]{:T(128)} %get-tuple-element.825), channel_id=1, replica_groups=mesh['gx'=8,'gy'=16] {'gx','gy'}, use_global_device_ids=true, to_apply=%region_6.6 | all-reduce | flops 1 | bytes 8 | tf_op jit(solution)/shard_map/while/body/eval_jaxpr/psum | solution.py:302
  1735.5 65.5 %psum.42 = f32[]{:T(128)} all-reduce(f32[]{:T(128)} %get-tuple-element.823), channel_id=1, replica_groups=mesh['gx'=8,'gy'=16] {'gx','gy'}, use_global_device_ids=true, to_apply=%region_4.4 | all-reduce | flops 1 | bytes 8 | tf_op jit(solution)/shard_map/while/body/eval_jaxpr/psum | solution.py:302
  1803.7 62.5 %psum.43 = f32[]{:T(128)} all-reduce(f32[]{:T(128)} %get-tuple-element.825), channel_id=1, replica_groups=mesh['gx'=8,'gy'=16] {'gx','gy'}, use_global_device_ids=true, to_apply=%region_6.6 | all-reduce | flops 1 | bytes 8 | tf_op jit(solution)/shard_map/while/body/eval_jaxpr/psum | solution.py:302
  1899.1 65.5 %psum.42 = f32[]{:T(128)} all-reduce(f32[]{:T(128)} %get-tuple-element.823), channel_id=1, replica_groups=mesh['gx'=8,'gy'=16] {'gx','gy'}, use_global_device_ids=true, to_apply=%region_4.4 | all-reduce | flops 1 | bytes 8 | tf_op jit(solution)/shard_map/while/body/eval_jaxpr/psum | solution.py:302
  1967.3 62.5 %psum.43 = f32[]{:T(128)} all-reduce(f32[]{:T(128)} %get-tuple-element.825), channel_id=1, replica_groups=mesh['gx'=8,'gy'=16] {'gx','gy'}, use_global_device_ids=true, to_apply=%region_6.6 | all-reduce | flops 1 | bytes 8 | tf_op jit(solution)/shard_map/while/body/eval_jaxpr/psum | solution.py:302
  (1159 shorter events, 737.8 us)
Async XLA Ops:
  2.9 10.3 collective-permute-start.4
  13.9 60.2 %collective-permute-start.6 = (f32[26,1,384]{2,1,0:T(1,128)}, f32[26,1,384]{2,1,0:T(1,128)}, u32[]{:S(2)}, u32[]{:S(2)}) collective-permute-start(f32[26,1,384]{2,1,0:T(1,128)} %get-tuple-element.590), channel_id=1, source_target_pairs={{0,1},{1,2},{2,3},{3,4},{4,5},{5,6},{6,7},{7,8},{8,9},{9,10},{10,1... | collective-permute-start | bytes 119816 | tf_op jit(solution)/shard_map/ppermute | solution.py:21
  18.1 56.1 %collective-permute-start.7 = (f32[26,1,384]{2,1,0:T(1,128)}, f32[26,1,384]{2,1,0:T(1,128)}, u32[]{:S(2)}, u32[]{:S(2)}) collective-permute-start(f32[26,1,384]{2,1,0:T(1,128)} %get-tuple-element.591), channel_id=1, source_target_pairs={{1,0},{2,1},{3,2},{4,3},{5,4},{6,5},{7,6},{8,7},{9,8},{10,9},{11,1... | collective-permute-start | bytes 119816 | tf_op jit(solution)/shard_map/ppermute | solution.py:23
  103.8 6.6 collective-permute-start.10
  167.2 51.5 %collective-permute-start.18 = (f32[18,1,256]{2,1,0:T(1,128)}, f32[18,1,256]{2,1,0:T(1,128)}, u32[]{:S(2)}, u32[]{:S(2)}) collective-permute-start(f32[18,1,256]{2,1,0:T(1,128)} %get-tuple-element.620), channel_id=1, source_target_pairs={{0,1},{1,2},{2,3},{3,4},{4,5},{5,6},{6,7},{7,8},{8,9},{9,10},{10,1... | collective-permute-start | bytes 55304 | tf_op jit(solution)/shard_map/ppermute | solution.py:21
  173.5 45.3 %collective-permute-start.19 = (f32[18,1,256]{2,1,0:T(1,128)}, f32[18,1,256]{2,1,0:T(1,128)}, u32[]{:S(2)}, u32[]{:S(2)}) collective-permute-start(f32[18,1,256]{2,1,0:T(1,128)} %get-tuple-element.621), channel_id=1, source_target_pairs={{1,0},{2,1},{3,2},{4,3},{5,4},{6,5},{7,6},{8,7},{9,8},{10,9},{11,1... | collective-permute-start | bytes 55304 | tf_op jit(solution)/shard_map/ppermute | solution.py:23
  234.0 8.7 collective-permute-start.20
  236.2 6.5 collective-permute-start.21
  243.5 11.0 collective-permute-start.22
  247.5 7.0 collective-permute-start.23
  296.3 24.1 %collective-permute-start.30 = (f32[10,1,128]{2,1,0:T(1,128)}, f32[10,1,128]{2,1,0:T(1,128)}, u32[]{:S(2)}, u32[]{:S(2)}) collective-permute-start(f32[10,1,128]{2,1,0:T(1,128)} %get-tuple-element.666), channel_id=1, source_target_pairs={{0,1},{1,2},{2,3},{3,4},{4,5},{5,6},{6,7},{7,8},{8,9},{9,10},{10,1... | collective-permute-start | bytes 15368 | tf_op jit(solution)/shard_map/ppermute | solution.py:21
  300.5 19.9 collective-permute-start.31
  408.5 15.9 collective-permute-start.2
  409.8 14.6 collective-permute-start.3
  571.9 15.9 collective-permute-start.2
  573.2 14.6 collective-permute-start.3
  735.7 15.9 collective-permute-start.2
  737.0 14.6 collective-permute-start.3
  899.3 15.9 collective-permute-start.2
  900.6 14.6 collective-permute-start.3
  1062.9 15.9 collective-permute-start.2
  1064.2 14.6 collective-permute-start.3
  1226.5 15.9 collective-permute-start.2
  1227.8 14.6 collective-permute-start.3
  1390.1 15.9 collective-permute-start.2
  1391.3 14.6 collective-permute-start.3
  1553.6 15.9 collective-permute-start.2
  1554.9 14.6 collective-permute-start.3
  1717.2 15.9 collective-permute-start.2
  1718.5 14.6 collective-permute-start.3
  1880.8 15.9 collective-permute-start.2
  1882.1 14.6 collective-permute-start.3
  (257 other events, 1596.4 us)
where the time goes:
time: 2180 us; the launch traced here: 2160 us
  blocking collectives  1350 us (62%)
  local copies, waits for them, and re-layouts  304 us (14%)
  starting transfers between devices  231 us (11%)
  other arithmetic  103 us (5%)
  matrix products  92.7 us (4%)
  waiting for transfers between devices  55.3 us (3%)
  loops' own time  22.8 us (1%)
    psum x21, blocking collectives, sum_spread(): return lax.psum(partial_sum, ('gx', 'gy'))  1350 us
    ppermute x42, starting transfers between devices, with_halo(): lax.ppermute(tail, axis, [(i, (i + 1) % count) for i in range(ends)])  156 us
    ppermute x42, starting transfers between devices, with_halo(): lax.ppermute(head, axis, [((i + 1) % count, i) for i in range(ends)])  74.9 us
    mul x58, local copies, waits for them, and re-layouts, spread_counts(): at_end * step_two[:, :, 2:][:, :, :, None]  67 us
    add x52, local copies, waits for them, and re-layouts, spread_counts(): step_two[:, :, 1:-1][:, :, :, None]  64.9 us
    mul x58, local copies, waits for them, and re-layouts, spread_counts(): at_start * step_two[:, :, :-2][:, :, :, None]  54.8 us
    ppermute x42, waiting for transfers between devices, with_halo(): lax.ppermute(head, axis, [((i + 1) % count, i) for i in range(ends)])  48 us
  transfers between devices with their start and end apart: 84, of which 26 were waited for; matrix products, arithmetic and copies ran while one was open for 11% of the time, Pallas kernels for 0%

commit v1 on v0

v1 whole, which is shorter than its diff:
```python
import functools

import jax
import jax.numpy as jnp
import numpy as np
from jax import lax
from jax.experimental import pallas as pl
from jax.experimental.pallas import tpu as pltpu
from jax.sharding import PartitionSpec as P

CG_ITERS = 10
VMEM = pl.BlockSpec(memory_space=pltpu.VMEM)
SMEM = pl.BlockSpec(memory_space=pltpu.SMEM)
F32 = jnp.float32


def gll_nodes(n):
    if n == 6:
        o, m = 0.7650553239294647, 0.2852315164806451
        points = [-1.0, -o, -m, m, o, 1.0]
        w = [1.0 / 15.0, 0.378474956297847, 0.5548583770354863]
        weights = w + w[::-1]
    elif n == 4:
        m = 0.4472135954999579
        points = [-1.0, -m, m, 1.0]
        weights = [1.0 / 6.0, 5.0 / 6.0, 5.0 / 6.0, 1.0 / 6.0]
    else:
        points, weights = [-1.0, 1.0], [1.0, 1.0]
    return np.array(points), np.array(weights)


def lagrange_tables(n):
    points, weights = gll_nodes(n)
    bary = np.array(
        [1.0 / np.prod([points[c] - points[o] for o in range(n) if o != c]) for c in range(n)]
    )
    deriv = np.zeros((n, n))
    for r in range(n):
        for c in range(n):
            if r != c:
                deriv[r, c] = bary[c] / bary[r] / (points[r] - points[c])
        deriv[r, r] = -np.sum(deriv[r])
    return deriv.T @ (weights[:, None] * deriv), weights


def interpolation(coarse, fine):
    xc, xf = gll_nodes(coarse)[0], gll_nodes(fine)[0]
    m = np.ones((fine, coarse))
    for r in range(fine):
        for c in range(coarse):
            for o in range(coarse):
                if o != c:
                    m[r, c] *= (xf[r] - xc[o]) / (xc[c] - xc[o])
    return m


def diag_table(n):
    s, w = lagrange_tables(n)
    d = np.diag(s)
    return (
        d[:, None, None] * w[None, :, None] * w[None, None, :]
        + w[:, None, None] * d[None, :, None] * w[None, None, :]
        + w[:, None, None] * w[None, :, None] * d[None, None, :]
    )


def cheb(n):
    s, w = lagrange_tables(n)
    r = np.abs(s).sum(axis=1)
    num = (
        r[:, None, None] * w[None, :, None] * w[None, None, :]
        + w[:, None, None] * r[None, :, None] * w[None, None, :]
        + w[:, None, None] * w[None, :, None] * r[None, None, :]
    )
    top = float(np.max(num / diag_table(n)))
    center, half = 0.5 * (top + 0.1 * top), 0.5 * (top - 0.1 * top)
    rho0 = half / center
    rho1 = 1.0 / (2.0 * center / half - rho0)
    return center, rho1 * rho0, 2.0 * rho1 / half


def lane_iota(rows=8):
    return lax.broadcasted_iota(jnp.int32, (rows, 128), 1)


def row_iota(rows=8):
    return lax.broadcasted_iota(jnp.int32, (rows, 128), 0)


def per(n):
    return n * n * (n // 2)


def ix(n, i, j, k):
    return (i * n + j) * (n // 2) + k


def at(slot, rows):
    start = slot * rows
    if not isinstance(start, int):
        start = pl.multiple_of(start, 8)
    return pl.ds(start, rows)


def ld(ref, slot, rows):
    return ref[at(slot, rows), :]


def st(ref, slot, rows, value):
    ref[at(slot, rows), :] = value


def swap(v):
    return pltpu.roll(v, 64, 1)


def cs_apply(m, v):
    no, ni = m.shape
    h = ni // 2
    e = [v[q] + v[ni - 1 - q] for q in range(h)]
    o = [v[q] - v[ni - 1 - q] for q in range(h)]
    out = [None] * no
    for p in range(no // 2):
        a = b = None
        for q in range(h):
            ce = float(0.5 * (m[p, q] + m[p, ni - 1 - q]))
            co = float(0.5 * (m[p, q] - m[p, ni - 1 - q]))
            ta, tb = e[q] * ce, o[q] * co
            a = ta if a is None else a + ta
            b = tb if b is None else b + tb
        out[p], out[no - 1 - p] = a + b, a - b
    return out


def cs_fold(m, v):
    no, ni = m.shape
    r = [swap(x) for x in v]
    out = []
    for p in range(no // 2):
        a = None
        for q in range(ni // 2):
            t = v[q] * float(m[p, q]) + r[q] * float(m[p, ni - 1 - q])
            a = t if a is None else a + t
        out.append(a)
    return out


def k_slab(n, src, a_src, acc, rows, emit):
    s, w = lagrange_tables(n)
    sh = s / w[:, None]
    kh, cnt = n // 2, per(n)
    base = a_src * cnt
    for j in range(n):
        for k in range(kh):
            line = cs_apply(sh, [ld(src, base + ix(n, i, j, k), rows) for i in range(n)])
            for i in range(n):
                st(acc, ix(n, i, j, k), rows, line[i])
    for i in range(n):
        v = [[ld(src, base + ix(n, i, j, k), rows) for k in range(kh)] for j in range(n)]
        t = [cs_fold(sh, v[j]) for j in range(n)]
        for k in range(kh):
            line = cs_apply(sh, [v[j][k] for j in range(n)])
            for j in range(n):
                total = t[j][k] + line[j] + ld(acc, ix(n, i, j, k), rows)
                t[j][k] = total * float(w[i] * w[j] * w[k])
        emit(i, t)


def z_partner(v):
    lane = lane_iota(v.shape[0])
    moved = jnp.where(lane < 64, pltpu.roll(v, 65, 1), pltpu.roll(v, 63, 1))
    return jnp.where((lane == 0) | (lane == 127), 0.0, moved)


def zy_sum(n, t):
    for j in range(n):
        t[j][0] = t[j][0] + z_partner(t[j][0])
    rows = t[0][0].shape[0]
    for k in range(n // 2):
        a, b = t[0][k], t[n - 1][k]
        t[0][k] = a + pltpu.roll(b, 1, 0)
        t[n - 1][k] = b + pltpu.roll(a, rows - 1, 0)
    return t


def put_plane(n, ref, base, i, t, rows):
    for j in range(n):
        for k in range(n // 2):
            st(ref, base + ix(n, i, j, k), rows, t[j][k])


def x_summed(n, ref, a, i, j, k, rows, low=True, high=True):
    cnt = per(n)
    v = ld(ref, a * cnt + ix(n, i, j, k), rows)
    if i == 0 and low is not False:
        v = v + ld(ref, (a - 1) * cnt + ix(n, n - 1, j, k), rows)
    if i == n - 1 and high is not False:
        v = v + ld(ref, (a + 1) * cnt + ix(n, 0, j, k), rows)
    return v


def cls(n, i):
    return 0 if i == 0 else (2 if i == n - 1 else 1)


def gslot(n, a, i, j, k):
    return ((a * 3 + cls(n, i)) * 3 + cls(n, j)) * 2 + (0 if k == 0 else 1)


def nodes(n):
    return [(i, j, k) for i in range(n) for j in range(n) for k in range(n // 2)]


def own_rows():
    row = row_iota()
    return (row >= 2) & (row < 6)


def own_sum(n, t_ref, out_ref):
    def body(a, carry):
        for i, j, k in nodes(n):
            st(out_ref, a * per(n) + ix(n, i, j, k), 8, x_summed(n, t_ref, a + 1, i, j, k, 8))
        return carry

    lax.fori_loop(0, 4, body, 0)


def zero_face(n, ref, a, i, rows):
    for j in range(n):
        for k in range(n // 2):
            st(ref, a * per(n) + ix(n, i, j, k), rows, jnp.zeros((rows, 128), F32))


def pack_column(n, src, a, dst, slot0):
    row = row_iota()
    cnt = per(n)
    for m in range(cnt // 2):
        u = ld(src, a * cnt + 2 * m, 8)
        v = ld(src, a * cnt + 2 * m + 1, 8)
        st(dst, slot0 + m, 8, jnp.where(row < 4, pltpu.roll(u, 6, 0), pltpu.roll(v, 2, 0)))


def own_row_lines(n, src, dst_lo, dst_hi):
    cnt = per(n)
    for a in range(4):
        dst_lo[pl.ds(a * cnt, cnt), :] = src[pl.ds(a * cnt * 8 + 2, cnt, stride=8), :]
        dst_hi[pl.ds(a * cnt, cnt), :] = src[pl.ds(a * cnt * 8 + 5, cnt, stride=8), :]


def split3(x):
    hi = x.astype(jnp.bfloat16)
    rest = x - hi.astype(F32)
    mid = rest.astype(jnp.bfloat16)
    return hi, mid, (rest - mid.astype(F32)).astype(jnp.bfloat16)


def exact_dot(x, perm):
    hi, mid, lo = split3(x)
    dot = functools.partial(jnp.dot, preferred_element_type=F32)
    return dot(hi, perm) + dot(mid, perm) + dot(lo, perm)


def layout_kernel(src_ref, perm_ref, s_ref, b_ref, ml_ref, mr_ref, lo_ref, hi_ref, y_ref, t_ref):
    y = exact_dot(src_ref[...], perm_ref[...])
    for k in range(3):
        y_ref[pl.ds(624 * k, 16), :] = jnp.zeros((16, 128), F32)
        y_ref[pl.ds(624 * k + 592, 32), :] = jnp.zeros((32, 128), F32)
        y_ref[pl.ds(624 * k + 16, 576), :] = y[:, 128 * k : 128 * k + 128]
    own = own_rows()
    n, cnt = 6, per(6)
    zero_face(n, t_ref, 0, n - 1, 8)
    zero_face(n, t_ref, 5, 0, 8)
    for a in range(4):
        for i in range(n):
            t = [[None] * 3 for _ in range(n)]
            for j in range(n):
                start = 16 + (a * 6 + i) * 24 + j - 12
                for k in range(3):
                    v = y_ref[pl.ds(624 * k + start, 8, stride=6), :]
                    v = jnp.where(own, v, 0.0)
                    st(s_ref, a * cnt + ix(n, i, j, k), 8, v)
                    t[j][k] = v
            put_plane(n, t_ref, (a + 1) * cnt, i, zy_sum(n, t), 8)
    own_sum(n, t_ref, b_ref)
    pack_column(n, b_ref, 0, ml_ref, 0)
    pack_column(n, b_ref, 3, mr_ref, 0)
    own_row_lines(n, b_ref, lo_ref, hi_ref)


def flags(ids_ref):
    gx, gy = ids_ref[0], ids_ref[1]
    one = lambda c: jnp.where(c, 1.0, 0.0).astype(F32)
    return one(gx > 0), one(gx < ids_ref[2] - 1), one(gy > 0), one(gy < ids_ref[3] - 1)


def y_line(n, h, own_line, fl, fr, left, right, b, dst, off, partial):
    cnt = per(n)
    q = cnt // n
    for t in range(h):
        dst[pl.ds(off + t * cnt, cnt), :] = fl * left[pl.ds(t * cnt * 4 + b, cnt, stride=4), :]
        dst[pl.ds(off + (4 + h + t) * cnt, cnt), :] = (
            fr * right[pl.ds(t * cnt * 4 + b, cnt, stride=4), :]
        )
    for a in range(4):
        dst[pl.ds(off + (h + a) * cnt, cnt), :] = own_line(a)
    if partial:
        for edge in (h, h + 4):
            lo = pl.ds(off + edge * cnt - q, q)
            hi = pl.ds(off + edge * cnt, q)
            total = dst[lo, :] + dst[hi, :]
            dst[lo, :] = total
            dst[hi, :] = total


def y_lines_kernel(n, ids_ref, lo_ref, hi_ref, left_ref, right_ref, dn_ref, up_ref):
    fl, fr, _, _ = flags(ids_ref)
    cnt = per(n)
    for b, src, dst in ((0, lo_ref, dn_ref), (3, hi_ref, up_ref)):
        line = lambda a, src=src: src[pl.ds(a * cnt, cnt), :]
        y_line(n, 1, line, fl, fr, left_ref, right_ref, b, dst, 0, True)


def unpack(n, h, a0, rows, r0, own, left, right, low, high, offs, fl, dst, partial):
    fleft, fright, flow, fhigh = fl
    oleft, olow = offs
    cnt = per(n)
    row = row_iota()
    keep = own_rows()
    shift = r0 - 2

    def place(v):
        v = jnp.where(keep, v, 0.0)
        if shift:
            v = pltpu.roll(v, shift, 0)
        if rows > 8:
            v = jnp.concatenate([v, jnp.zeros((rows - 8, 128), F32)], axis=0)
        return v

    def own_body(a, carry):
        for m in range(cnt):
            st(dst, (a0 + a) * cnt + m, rows, place(ld(own, a * cnt + m, 8)))
        return carry

    lax.fori_loop(0, 4, own_body, 0)
    for src, f, first in ((left, fleft, a0 - h), (right, fright, a0 + 4)):

        def ring_body(t, carry, src=src, f=f, first=first):
            for m in range(cnt // 2):
                v = f * ld(src, oleft // 8 + t * (cnt // 2) + m, 8)
                st(dst, (first + t) * cnt + 2 * m, rows, place(pltpu.roll(v, 2, 0)))
                st(dst, (first + t) * cnt + 2 * m + 1, rows, place(pltpu.roll(v, 6, 0)))
            return carry

        lax.fori_loop(0, h, ring_body, 0)
    if partial:
        for edge in (a0, a0 + 4):
            for j in range(n):
                for k in range(n // 2):
                    lo = (edge - 1) * cnt + ix(n, n - 1, j, k)
                    hi = edge * cnt + ix(n, 0, j, k)
                    total = ld(dst, lo, rows) + ld(dst, hi, rows)
                    st(dst, lo, rows, total)
                    st(dst, hi, rows, total)
    wide = 4 + 2 * h
    for src, f, first in ((low, flow, r0 - h), (high, fhigh, r0 + 4)):
        for t in range(h):
            for a in range(wide):
                line = f * src[pl.ds(olow + (t * wide + a) * cnt, cnt), :]
                dst[pl.ds((a0 - h + a) * cnt * rows + first + t, cnt, stride=rows), :] = line
    if partial:
        row = row_iota(rows)
        to_hi = (row == r0) | (row == r0 + 4)
        to_lo = (row == r0 - 1) | (row == r0 + 3)

        def y_body(a, carry):
            for i in range(n):
                for k in range(n // 2):
                    lo = (a0 - h + a) * cnt + ix(n, i, 0, k)
                    hi = (a0 - h + a) * cnt + ix(n, i, n - 1, k)
                    u, v = ld(dst, lo, rows), ld(dst, hi, rows)
                    st(dst, lo, rows, u + jnp.where(to_hi, pltpu.roll(v, 1, 0), 0.0))
                    st(dst, hi, rows, v + jnp.where(to_lo, pltpu.roll(u, rows - 1, 0), 0.0))
            return carry

        lax.fori_loop(0, wide, y_body, 0)


def down_smooth(n, b_ref, g_ref, g0, u_ref, t_ref, acc_ref, z_ref):
    center, ca, cb = cheb(n)
    d = diag_table(n)
    cnt = per(n)
    own = own_rows()

    def first(a, carry):
        for i, j, k in nodes(n):
            s = a * cnt + ix(n, i, j, k)
            g = ld(g_ref, gslot(n, a + g0, i, j, k), 8)
            st(u_ref, s, 8, g * ld(b_ref, s, 8) * float(1.0 / (d[i, j, k] * center)))
        return carry

    lax.fori_loop(0, 6, first, 0)

    def second(a, carry):
        put = lambda i, t: put_plane(n, t_ref, a * cnt, i, zy_sum(n, t), 8)
        k_slab(n, u_ref, a, acc_ref, 8, put)
        return carry

    lax.fori_loop(0, 6, second, 0)

    def third(a, carry):
        for i, j, k in nodes(n):
            s = (a + 1) * cnt + ix(n, i, j, k)
            g = ld(g_ref, gslot(n, a + 1 + g0, i, j, k), 8)
            r = ld(b_ref, s, 8) - x_summed(n, t_ref, a + 1, i, j, k, 8)
            z = ld(u_ref, s, 8) * (1.0 + ca) + g * r * float(cb / d[i, j, k])
            st(z_ref, a * cnt + ix(n, i, j, k), 8, jnp.where(own, z, 0.0))
        return carry

    lax.fori_loop(0, 4, third, 0)


def down_residual(n, nc, s_ref, z_ref, g_ref, g0, t_ref, acc_ref, w1_ref, w2_ref, rp_ref, emit):
    cnt = per(n)
    kh, kc = n // 2, nc // 2
    m = interpolation(nc, n).T
    zero_face(n, t_ref, 0, n - 1, 8)
    zero_face(n, t_ref, 5, 0, 8)

    def body(a, carry):
        def put(i, t):
            for j in range(n):
                for k in range(kh):
                    t[j][k] = ld(s_ref, a * cnt + ix(n, i, j, k), 8) - t[j][k]
                    g = ld(g_ref, gslot(n, a + 1 + g0, i, j, k), 8)
                    st(w1_ref, ix(n, i, j, k), 8, jnp.where(g > 0.0, t[j][k], 0.0))
            put_plane(n, t_ref, (a + 1) * cnt, i, zy_sum(n, t), 8)

        k_slab(n, z_ref, a, acc_ref, 8, put)
        for j in range(n):
            for k in range(kh):
                line = cs_apply(m, [ld(w1_ref, ix(n, i, j, k), 8) for i in range(n)])
                for i in range(nc):
                    st(w2_ref, ix(n, i, j, k), 8, line[i])
        coarse = []
        for i in range(nc):
            cols = []
            for k in range(kh):
                cols.append(cs_apply(m, [ld(w2_ref, ix(n, i, j, k), 8) for j in range(n)]))
            plane = [cs_fold(m, [cols[k][j] for k in range(kh)]) for j in range(nc)]
            emit(a, i, plane)
        return carry

    lax.fori_loop(0, 4, body, 0)
    own_sum(n, t_ref, rp_ref)


def fine_down_kernel(
    ids_ref, s_ref, bp_ref, left_ref, right_ref, low_ref, high_ref, g_ref,
    z_ref, rp_ref, ml_ref, mr_ref, s3_ref, b3_ref, m3l_ref, m3r_ref, lo3_ref, hi3_ref,
    b_ref, u_ref, t_ref, acc_ref, w1_ref, w2_ref, t3_ref,
):
    fl = flags(ids_ref)
    unpack(6, 1, 1, 8, 2, bp_ref, left_ref, right_ref, low_ref, high_ref, (0, 0), fl, b_ref, True)
    down_smooth(6, b_ref, g_ref, 1, u_ref, t_ref, acc_ref, z_ref)
    c3 = per(4)
    zero_face(4, t3_ref, 0, 3, 8)
    zero_face(4, t3_ref, 5, 0, 8)

    def emit(a, i, plane):
        put_plane(4, s3_ref, a * c3, i, plane, 8)
        put_plane(4, t3_ref, (a + 1) * c3, i, zy_sum(4, plane), 8)

    down_residual(
        6, 4, s_ref, z_ref, g_ref, 1, t_ref, acc_ref, w1_ref, w2_ref, rp_ref, emit
    )
    own_sum(4, t3_ref, b3_ref)
    pack_column(4, b3_ref, 0, m3l_ref, 0)
    pack_column(4, b3_ref, 3, m3r_ref, 0)
    own_row_lines(4, b3_ref, lo3_ref, hi3_ref)
    pack_column(6, rp_ref, 0, ml_ref, 0)
    pack_column(6, rp_ref, 3, mr_ref, 0)


X5, X3R, X3Z = 108 * 4, 3 * 32 * 4, 2 * 32 * 4
Y5, Y3R, Y3Z = 6 * 108, 3 * 10 * 32, 2 * 8 * 32


def middle_down_kernel(
    ids_ref, s_ref, bp_ref, left_ref, right_ref, low_ref, high_ref, g_ref, m5l_ref, m5r_ref,
    z_ref, rp_ref, ml_ref, mr_ref, block_ref,
    b_ref, u_ref, t_ref, acc_ref, w1_ref, w2_ref, c_ref,
):
    fl = flags(ids_ref)
    unpack(4, 1, 1, 8, 2, bp_ref, left_ref, right_ref, low_ref, high_ref, (0, 0), fl, b_ref, True)
    down_smooth(4, b_ref, g_ref, 1, u_ref, t_ref, acc_ref, z_ref)

    def emit(a, i, plane):
        lane = lane_iota()
        line = []
        for j in range(2):
            v = plane[j][0]
            line.append(swap(v) + jnp.where(lane < 63, pltpu.roll(v, 127, 1), 0.0))
        st(c_ref, a * 2 + i, 8, line[0] + pltpu.roll(line[1], 1, 0))

    down_residual(
        4, 2, s_ref, z_ref, g_ref, 1, t_ref, acc_ref, w1_ref, w2_ref, rp_ref, emit
    )
    planes = []
    for a in range(5):
        v = None
        if a < 4:
            v = ld(c_ref, a * 2, 8)
        if a > 0:
            u = ld(c_ref, (a - 1) * 2 + 1, 8)
            v = u if v is None else v + u
        planes.append(v)
    lane = lane_iota()
    block_ref[...] = jnp.zeros((16, 128), F32)
    for p in range(3):
        v = planes[2 * p]
        other = swap(planes[2 * p + 1]) if p < 2 else jnp.zeros((8, 128), F32)
        v = jnp.where(lane < 64, v, other)
        block_ref[pl.ds(5 * p, 5), :] = v[2:7]
    ml_ref[pl.ds(0, X5), :] = m5l_ref[...]
    mr_ref[pl.ds(0, X5), :] = m5r_ref[...]
    for t in range(3):
        pack_column(4, rp_ref, t, ml_ref, X5 // 8 + t * 16)
        pack_column(4, rp_ref, 1 + t, mr_ref, X5 // 8 + t * 16)
    for t in range(2):
        pack_column(4, z_ref, t, ml_ref, (X5 + X3R) // 8 + t * 16)
        pack_column(4, z_ref, 2 + t, mr_ref, (X5 + X3R) // 8 + t * 16)


def up_lines_kernel(ids_ref, r5_ref, r3_ref, z3_ref, left_ref, right_ref, dn_ref, up_ref):
    fl, fr, _, _ = flags(ids_ref)
    for dst, r5row, r3rows, z3rows in (
        (dn_ref, 0, (0, 1, 2), (0, 1)),
        (up_ref, 3, (1, 2, 3), (2, 3)),
    ):
        def line(src, cnt, b):
            return lambda a: src[pl.ds(a * cnt * 8 + 2 + b, cnt, stride=8), :]

        def part(ref, start, size):
            return ref.at[pl.ds(start, size), :]

        y_line(
            6, 1, line(r5_ref, 108, r5row), fl, fr, part(left_ref, 0, X5), part(right_ref, 0, X5),
            r5row, dst, 0, True,
        )
        for t, b in enumerate(r3rows):
            y_line(
                4, 3, line(r3_ref, 32, b), fl, fr, part(left_ref, X5, X3R),
                part(right_ref, X5, X3R), b, dst, Y5 + t * 320, True,
            )
        for t, b in enumerate(z3rows):
            y_line(
                4, 2, line(z3_ref, 32, b), fl, fr, part(left_ref, X5 + X3R, X3Z),
                part(right_ref, X5 + X3R, X3Z), b, dst, Y5 + Y3R + t * 256, False,
            )


def coarse_kernel(
    ids_ref, gath_ref, w_ref, perm_ref, win_ref, out_ref, x_ref, r_ref, p_ref, q_ref, o_ref
):
    gy = ids_ref[1]
    gx = ids_ref[0]
    lane = lane_iota(72)
    body = pl.ds(8, 72)
    for ref in (x_ref, r_ref, p_ref, q_ref):
        ref[...] = jnp.zeros(ref.shape, F32)
    lane16 = lane_iota(16)
    for g in range(4):
        for i in range(5):
            for r in range(5):
                lo = gath_ref[pl.ds((g * 16) * 16 + (i // 2) * 5 + r, 16, stride=16), :]
                hi = gath_ref[
                    pl.ds(((7 - g) * 16) * 16 + ((4 - i) // 2) * 5 + r, 16, stride=16), :
                ]
                if i % 2 == 0:
                    v = jnp.where(lane16 < 64, lo, swap(hi))
                else:
                    v = jnp.where(lane16 < 64, swap(lo), hi)
                rows = pl.ds(8 + r, 16, stride=4)
                r_ref[4 * g + i, rows, :] = r_ref[4 * g + i, rows, :] + v
    mid = r_ref[16, body, :]
    r_ref[16, body, :] = mid + swap(mid)

    def fold(v):
        return jnp.sum(v.reshape(9, 8, 128), axis=0)

    acc = jnp.zeros((8, 128), F32)
    for la in range(17):
        v = jnp.where(w_ref[la] > 0.0, r_ref[la, body, :], 0.0)
        r_ref[la, body, :] = v
        acc = acc + fold(v * v) * (0.5 if la == 16 else 1.0)
    rr = jnp.sum(acc)

    kk = lane & 63
    zdn = jnp.where(kk == 0, 0.0, jnp.where(kk == 63, 1.0, 0.5)).astype(F32)
    zup = jnp.where(kk == 63, 0.0, 0.5).astype(F32)
    brow = row_iota(72)
    yco = jnp.where((brow == 0) | (brow == 64), 1.0, 0.5).astype(F32)

    def iterate(_, carry):
        rr, beta = carry
        for la in range(17):
            p_ref[la, body, :] = r_ref[la, body, :] + beta * p_ref[la, body, :]
        acc = jnp.zeros((8, 128), F32)
        for la in range(17):
            v = p_ref[la, body, :]
            if la == 0:
                xs = p_ref[1, body, :]
            elif la == 16:
                u = p_ref[15, body, :]
                xs = 0.5 * (u + swap(u))
            else:
                xs = 0.5 * (p_ref[la - 1, body, :] + p_ref[la + 1, body, :])
            ys = yco * (p_ref[la, pl.ds(7, 72), :] + p_ref[la, pl.ds(9, 72), :])
            zs = zdn * pltpu.roll(v, 1, 1) + zup * pltpu.roll(v, 127, 1)
            q = w_ref[la] * (3.0 * v - xs - ys - zs)
            q_ref[la, body, :] = q
            acc = acc + fold(v * q) * (0.5 if la == 16 else 1.0)
        step = rr / jnp.sum(acc)
        acc = jnp.zeros((8, 128), F32)
        for la in range(17):
            x_ref[la, body, :] = x_ref[la, body, :] + step * p_ref[la, body, :]
            v = r_ref[la, body, :] - step * q_ref[la, body, :]
            r_ref[la, body, :] = v
            acc = acc + fold(v * v) * (0.5 if la == 16 else 1.0)
        new = jnp.sum(acc)
        return new, new / rr

    lax.fori_loop(0, CG_ITERS, iterate, (rr, jnp.zeros((), F32)))

    lane24 = lane_iota(24)
    row0 = pl.multiple_of(4 + 4 * gy, 4)
    for t in range(13):
        a = jnp.clip(4 * gx - 4 + t, 0, 32)
        v = x_ref[jnp.minimum(a, 32 - a), pl.ds(row0, 24), :]
        v = jnp.where(a > 16, swap(v), v)
        bottom = jnp.where(lane24 == 0, 0.0, pltpu.roll(v, 1, 1))
        win_ref[t] = jnp.where(lane24 < 64, bottom, swap(v))
    for a in range(4):
        for i in range(2):
            for j in range(2):
                o_ref[pl.ds((2 * a + i) * 8 + j, 4, stride=2), :] = win_ref[
                    4 + a + i, pl.ds(4 + j, 4), :
                ]
    out_ref[...] = exact_dot(o_ref[...], perm_ref[...])


def up_smooth(n, wide, rows, v_ref, r_ref, g_ref, u_ref, t_ref, acc_ref, finish):
    center, ca, cb = cheb(n)
    d = diag_table(n)
    cnt = per(n)

    def apply_to(src, lo, hi):
        def body(a, carry):
            put = lambda i, t: put_plane(n, t_ref, a * cnt, i, zy_sum(n, t), rows)
            k_slab(n, src, a, acc_ref, rows, put)
            return carry

        lax.fori_loop(lo, hi, body, 0)

    apply_to(v_ref, 0, wide)

    def first(a, carry):
        for i, j, k in nodes(n):
            s = a * cnt + ix(n, i, j, k)
            r = ld(r_ref, s, rows) - x_summed(n, t_ref, a, i, j, k, rows)
            st(r_ref, s, rows, r)
            g = ld(g_ref, gslot(n, a, i, j, k), rows)
            st(u_ref, s, rows, g * r * float(1.0 / (d[i, j, k] * center)))
        return carry

    lax.fori_loop(1, wide - 1, first, 0)
    apply_to(u_ref, 1, wide - 1)

    def second(a, carry):
        for i, j, k in nodes(n):
            s = a * cnt + ix(n, i, j, k)
            r = ld(r_ref, s, rows) - x_summed(n, t_ref, a, i, j, k, rows)
            g = ld(g_ref, gslot(n, a, i, j, k), rows)
            x = ld(v_ref, s, rows) + ld(u_ref, s, rows) * (1.0 + ca)
            finish(a, i, j, k, x + g * r * float(cb / d[i, j, k]))
        return carry

    lax.fori_loop(2, wide - 2, second, 0)


def up_kernel(
    ids_ref, win_ref, r5p_ref, z5_ref, r3p_ref, z3p_ref, left_ref, right_ref, low_ref, high_ref,
    g5_ref, g3_ref, perm_ref, out_ref,
    v3_ref, r3_ref, z3_ref, u3_ref, t3_ref, a3_ref, v5_ref, r5_ref, u5_ref, t5_ref, a5_ref,
    w1_ref, w2_ref, y_ref,
):
    fl = flags(ids_ref)
    c3, c5 = per(4), per(6)

    def take(n, h, a0, rows, r0, own, offs, dst, partial):
        unpack(
            n, h, a0, rows, r0, own, left_ref, right_ref, low_ref, high_ref, offs, fl, dst, partial
        )

    take(6, 1, 2, 8, 2, r5p_ref, (0, 0), r5_ref, True)
    take(4, 3, 4, 16, 4, r3p_ref, (X5, Y5), r3_ref, True)
    take(4, 2, 4, 16, 4, z3p_ref, (X5 + X3R, Y5 + Y3R), z3_ref, False)

    m = interpolation(2, 4)

    def prolong1(a, carry):
        corner = [[[win_ref[a + i, pl.ds(j, 16), :]] for j in range(2)] for i in range(2)]
        along = [cs_apply(m, [corner[0][j][0], corner[1][j][0]]) for j in range(2)]
        for i in range(4):
            line = cs_apply(m, [along[0][i], along[1][i]])
            for j in range(4):
                v = cs_fold(m, [line[j]])
                for k in range(2):
                    g = ld(g3_ref, gslot(4, a, i, j, k), 16)
                    st(v3_ref, a * c3 + ix(4, i, j, k), 16, jnp.where(g > 0.0, v[k], 0.0))
        return carry

    lax.fori_loop(0, 12, prolong1, 0)

    def finish3(a, i, j, k, x):
        s = a * c3 + ix(4, i, j, k)
        st(z3_ref, s, 16, ld(z3_ref, s, 16) + x)

    up_smooth(4, 12, 16, v3_ref, r3_ref, g3_ref, u3_ref, t3_ref, a3_ref, finish3)

    m5 = interpolation(4, 6)

    def prolong3(a, carry):
        for j in range(4):
            for k in range(2):
                src = []
                for i in range(4):
                    v = ld(z3_ref, (a + 2) * c3 + ix(4, i, j, k), 16)
                    src.append(v[2:10])
                line = cs_apply(m5, src)
                for i in range(6):
                    st(w1_ref, (i * 4 + j) * 2 + k, 8, line[i])
        for i in range(6):
            cols = []
            for k in range(2):
                cols.append(cs_apply(m5, [ld(w1_ref, (i * 4 + j) * 2 + k, 8) for j in range(4)]))
            for j in range(6):
                v = cs_fold(m5, [cols[k][j] for k in range(2)])
                for k in range(3):
                    g = ld(g5_ref, gslot(6, a, i, j, k), 8)
                    st(v5_ref, a * c5 + ix(6, i, j, k), 8, jnp.where(g > 0.0, v[k], 0.0))
        return carry

    lax.fori_loop(0, 8, prolong3, 0)

    def finish5(a, i, j, k, x):
        s = ix(6, i, j, k)
        v = ld(z5_ref, (a - 2) * c5 + s, 8) + x
        start = ((a - 2) * 6 + i) * 24 + j
        y_ref[pl.ds(576 * k + start, 4, stride=6), :] = v[2:6]

    up_smooth(6, 8, 8, v5_ref, r5_ref, g5_ref, u5_ref, t5_ref, a5_ref, finish5)
    y = jnp.concatenate([y_ref[pl.ds(576 * k, 576), :] for k in range(3)], axis=1)
    out_ref[...] = exact_dot(y, perm_ref[...])


def class_maps(heights, gx, gy, ring, rows, r0):
    na, nb = heights.shape
    w = 4 + 2 * ring + 2
    pad = ((ring + 1, ring + 1), (ring + 1, ring + 1))
    start = (4 * gx, 4 * gy)
    h = lax.dynamic_slice(jnp.pad(heights, pad), start, (w, w))
    e = lax.dynamic_slice(jnp.pad(jnp.ones((na, nb), F32), pad), start, (w, w))
    ax = jnp.arange(w) + 4 * gx - ring - 1
    ay = jnp.arange(w) + 4 * gy - ring - 1
    fx = ((ax >= 0) & (ax < na)).astype(F32)
    fy = ((ay >= 0) & (ay < nb)).astype(F32)
    hx = jnp.stack([jnp.maximum(h[:-2], h[1:-1]), h[1:-1], jnp.maximum(h[1:-1], h[2:])], 1)
    hxy = jnp.stack(
        [
            jnp.maximum(hx[:, :, :-2], hx[:, :, 1:-1]),
            hx[:, :, 1:-1],
            jnp.maximum(hx[:, :, 1:-1], hx[:, :, 2:]),
        ],
        2,
    )
    own = e[1:-1, 1:-1][:, None, None, :]
    hxy = jnp.where(own > 0.0, hxy, 1000)

    def inv(f):
        return jnp.stack([1.0 / (1.0 + f[:-2]), jnp.ones_like(f[1:-1]), 1.0 / (1.0 + f[2:])], 1)

    exy = inv(fx)[:, :, None, None] * inv(fy).T[None, None, :, :]
    extra = rows - (w - 2)
    hxy = jnp.pad(hxy, ((0, 0), (0, 0), (0, 0), (0, extra)), constant_values=1000)
    exy = jnp.pad(exy, ((0, 0), (0, 0), (0, 0), (0, extra)))
    lane = jnp.arange(128)
    c = lane & 63
    bound = jnp.stack([jnp.where(lane < 64, c - 1, c), c])
    zfac = jnp.stack([jnp.where(lane == 127, 1.0, 0.5), jnp.ones(128)]).astype(F32)
    g = jnp.where(
        bound[None, None, None, :, None, :] >= hxy[:, :, :, None, :, None],
        exy[:, :, :, None, :, None] * zfac[None, None, None, :, None, :],
        0.0,
    )
    return g.reshape(-1, 128)


def coarse_weight(heights):
    na, nb = heights.shape
    h = jnp.pad(heights, 1)
    hn = jnp.maximum(h[:-1], h[1:])
    hn = jnp.maximum(hn[:, :-1], hn[:, 1:])
    half = na // 2
    hn = jnp.stack([hn[: half + 1], hn[half:][::-1]], 2)
    hn = jnp.pad(hn, ((0, 0), (0, 72 - nb - 1), (0, 0)), constant_values=1000)
    hn = jnp.repeat(hn, 64, axis=2)
    la = jnp.arange(half + 1)
    b = jnp.arange(72)
    kk = jnp.arange(128) & 63
    ex = jnp.where(la == 0, 1.0, 2.0)[:, None, None]
    ey = jnp.where((b == 0) | (b == nb), 1.0, 2.0)[None, :, None]
    ez = jnp.where(kk == 63, 1.0, 2.0)[None, None, :]
    return jnp.where(kk[None, None, :] >= hn, 0.5 * ex * ey * ez, 0.0).astype(F32)


def perm_in():
    m = np.zeros((384, 384), np.float32)
    for z in range(384):
        c, k = divmod(z, 6)
        m[z, k * 128 + c if k < 3 else (5 - k) * 128 + 64 + c] = 1.0
    return m


def perm_coarse():
    m = np.zeros((128, 128), np.float32)
    for c in range(64):
        m[c, 2 * c] = 1.0
        m[64 + c, 2 * c + 1] = 1.0
    return m


def call(kernel, outs, ins, scratch):
    return pl.pallas_call(
        kernel,
        out_shape=[jax.ShapeDtypeStruct(s, F32) for s in outs],
        in_specs=ins,
        out_specs=[VMEM] * len(outs),
        scratch_shapes=[pltpu.VMEM(s, F32) for s in scratch],
        compiler_params=pltpu.CompilerParams(vmem_limit_bytes=56 * 1024 * 1024),
    )


def both_ways(axis, to_low, to_high):
    n = lax.axis_size(axis)
    from_low = lax.ppermute(to_high, axis, [(i, (i + 1) % n) for i in range(n)])
    from_high = lax.ppermute(to_low, axis, [(i, (i - 1) % n) for i in range(n)])
    return from_low, from_high


def per_device(source, heights):
    gx, gy = lax.axis_index("gx"), lax.axis_index("gy")
    nx, ny = lax.axis_size("gx"), lax.axis_size("gy")
    ids = jnp.stack([gx, gy, nx, ny]).astype(jnp.int32)
    g5 = class_maps(heights, gx, gy, 2, 8, 2)
    g3d = class_maps(heights, gx, gy, 2, 8, 2)
    g3 = class_maps(heights, gx, gy, 4, 16, 4)
    cw = coarse_weight(heights)
    pin = jnp.asarray(perm_in(), jnp.bfloat16)
    pout = jnp.asarray(perm_in().T, jnp.bfloat16)
    pc = jnp.asarray(perm_coarse(), jnp.bfloat16)

    def f(n, a):
        return (a * per(n) * 8, 128)

    s5, b5p, ml, mr, lo, hi = call(
        layout_kernel,
        [f(6, 4), f(6, 4), (432, 128), (432, 128), (432, 128), (432, 128)],
        [VMEM] * 2,
        [(1872, 128), f(6, 6)],
    )(source.reshape(576, 384), pin)
    left, right = both_ways("gx", ml, mr)
    dn, up = call(
        functools.partial(y_lines_kernel, 6), [(648, 128)] * 2, [SMEM] + [VMEM] * 4, []
    )(ids, lo, hi, left, right)
    low, high = both_ways("gy", dn, up)
    z5, r5p, m5l, m5r, s3, b3p, ml, mr, lo, hi = call(
        fine_down_kernel,
        [f(6, 4), f(6, 4), (432, 128), (432, 128), f(4, 4), f(4, 4)] + [(128, 128)] * 4,
        [SMEM] + [VMEM] * 7,
        [f(6, 6), f(6, 6), f(6, 6), f(6, 1), f(6, 1), f(6, 1), f(4, 6)],
    )(ids, s5, b5p, left, right, low, high, g5)
    left, right = both_ways("gx", ml, mr)
    dn, up = call(
        functools.partial(y_lines_kernel, 4), [(192, 128)] * 2, [SMEM] + [VMEM] * 4, []
    )(ids, lo, hi, left, right)
    low, high = both_ways("gy", dn, up)
    xr, yr = X5 + X3R + X3Z, Y5 + Y3R + Y3Z
    z3, r3p, ml, mr, block = call(
        middle_down_kernel,
        [f(4, 4), f(4, 4), (xr, 128), (xr, 128), (16, 128)],
        [SMEM] + [VMEM] * 9,
        [f(4, 6), f(4, 6), f(4, 6), f(4, 1), f(4, 1), f(4, 1), (64, 128)],
    )(ids, s3, b3p, left, right, low, high, g3d, m5l, m5r)
    every = jnp.broadcast_to(block[None], (nx * ny, 16, 128))
    gath = lax.all_to_all(every, ("gx", "gy"), 0, 0).reshape(nx * ny * 16, 128)
    left, right = both_ways("gx", ml, mr)
    dn, up = call(up_lines_kernel, [(yr, 128)] * 2, [SMEM] + [VMEM] * 5, [])(
        ids, r5p, r3p, z3, left, right
    )
    low, high = both_ways("gy", dn, up)
    win, coarse = call(
        coarse_kernel,
        [(13, 24, 128), (64, 128)],
        [SMEM] + [VMEM] * 3,
        [(17, 88, 128)] * 4 + [(64, 128)],
    )(ids, gath, cw, pc)

    def f16(a):
        return (a * per(4) * 16, 128)

    (out,) = call(
        up_kernel,
        [(576, 384)],
        [SMEM] + [VMEM] * 12,
        [f16(12), f16(12), f16(12), f16(12), f16(12), f16(1)]
        + [f(6, 8), f(6, 8), f(6, 8), f(6, 8), f(6, 1), f(6, 1), f(6, 1), (1728, 128)],
    )(ids, win, r5p, z5, r3p, z3, left, right, low, high, g5, g3, pout)
    return out.reshape(24, 24, 384), coarse.reshape(8, 8, 128)


def solution(mesh):
    spec = P("gx", "gy", None)
    return jax.shard_map(
        per_device, mesh=mesh, in_specs=(spec, P()), out_specs=(spec, spec), check_vma=False
    )
```

time: 2180 us -> 165 us (0.08)
  blocking collectives: 1350 us -> 0 us
  local copies, waits for them, and re-layouts: 304 us -> 9.6 us
  starting transfers between devices: 231 us -> 28.4 us
  other arithmetic: 103 us -> 8.84 us
  matrix products: 92.7 us -> 0 us
  Pallas kernels: 0 us -> 70.2 us
  loops' own time: 22.8 us -> 0 us
    psum x21 -> x0, blocking collectives: 1350 us -> none  [sum_spread(): return lax.psum(partial_sum, ('gx', 'gy'))]
    ppermute x84 -> x12, starting transfers between devices: 231 us -> 23 us  [the longest x6 14.4 us: both_ways(): from_high = lax.ppermute(to_low, axis, [(i, (i - 1) % n) for i in range(n)])]
    mul x144 -> x4, local copies, waits for them, and re-layouts: 129 us -> 0.37 us  [class_maps(): exy[:, :, :, None, :, None] * zfac[None, None, None, :, None, :]]
    dot_general x66 -> x0, matrix products: 92.7 us -> none  [the longest x22 33.2 us: along_first(): jnp.einsum('ip,xpr->xir', jnp.asarray(matrix, jnp.float32), shaped, preci...]
    pallas_call x0 -> x8, Pallas kernels: none -> 70.2 us  [the longest x1 27.6 us: per_device(): call(up_kernel, [(576, 384)], [SMEM] + [VMEM] * 12, [f16(12), f16(12), f1...]
    add x62 -> x0, local copies, waits for them, and re-layouts: 67.7 us -> none  [the longest x52 64.9 us: spread_counts(): step_two[:, :, 1:-1][:, :, :, None]]
    reshape x63 -> x1, local copies, waits for them, and re-layouts: 48 us -> 0.69 us  [coarse_weight(): hn = jnp.repeat(hn, 64, axis=2)]
    add x63 -> x0, other arithmetic: 43 us -> none  [the longest x10 14.1 us: iterate(): direction = residual_now + norm_next / norm_now * direction]
  transfers between devices with their start and end apart: 84 -> 13, of which waited for: 26 -> 8; matrix products, arithmetic and copies ran while one was open for 11% -> 8% of each run, Pallas kernels for 0% -> 7%
where the time goes in v1:
time: 165 us; the launch traced here: 164 us
  Pallas kernels  70.2 us (43%)
  waiting for transfers between devices  46 us (28%)
  starting transfers between devices  28.4 us (17%)
  local copies, waits for them, and re-layouts  9.6 us (6%)
  other arithmetic  8.84 us (5%)
    pallas_call x1, Pallas kernels, per_device(): call(up_kernel, [(576, 384)], [SMEM] + [VMEM] * 12, [f16(12), f16(12), f1...  27.6 us
    all_to_all x1, waiting for transfers between devices, per_device(): gath = lax.all_to_all(every, ('gx', 'gy'), 0, 0).reshape(nx * ny * 16, 128)  23.5 us
    ppermute x6, waiting for transfers between devices, both_ways(): from_low = lax.ppermute(to_high, axis, [(i, (i + 1) % n) for i in range(n)])  17 us
    ppermute x6, starting transfers between devices, both_ways(): from_high = lax.ppermute(to_low, axis, [(i, (i - 1) % n) for i in range(n)])  14.4 us
    pallas_call x1, Pallas kernels, per_device(): call(fine_down_kernel, [f(6, 4), f(6, 4), (432, 128), (432, 128), f(4, 4)...  12.9 us
    pallas_call x1, Pallas kernels, per_device(): call(coarse_kernel, [(13, 24, 128), (64, 128)], [SMEM] + [VMEM] * 3, [(17...  11.6 us
    ppermute x6, starting transfers between devices, both_ways(): from_low = lax.ppermute(to_high, axis, [(i, (i + 1) % n) for i in range(n)])  8.63 us
    pallas_call x1, Pallas kernels, per_device(): call(middle_down_kernel, [f(4, 4), f(4, 4), (xr, 128), (xr, 128), (16, 12...  5.79 us
  transfers between devices with their start and end apart: 13, of which 8 were waited for; matrix products, arithmetic and copies ran while one was open for 8% of the time, Pallas kernels for 7%

profile of v1, /device:TPU:1, one launch (start us, length us, event | category | flops | bytes accessed | tf_op | source)
XLA Modules:
  0.0 164.0 jit_solution(14070392132591970304)
XLA Ops:
  0.6 4.8 %shard_map.68 = (f32[3456,128]{1,0:T(8,128)}, f32[3456,128]{1,0:T(8,128)}, f32[432,128]{1,0:T(8,128)}, f32[432,128]{1,0:T(8,128)}, f32[432,128]{1,0:T(8,128)}, /*index=5*/f32[432,128]{1,0:T(8,128)}) custom-call(f32[576,384]{1,0:T(8,128)} %bitcast.72, bf16[384,384]{1,0:T(8,128)(2,1)} %constant.24.clone.perm_ref), custom_call_target="tpu_custom_call" | custom-call | tf_op jit(solution)/shard_map/pallas_call | solution.py:876
  5.4 2.6 %collective-permute-start = (f32[432,128]{1,0:T(8,128)}, f32[432,128]{1,0:T(8,128)S(1)}, u32[]{:S(2)}, u32[]{:S(2)}) collective-permute-start(f32[432,128]{1,0:T(8,128)} %get-tuple-element.33), channel_id=1, source_target_pairs={{0,16},{16,32},{32,48},{48,64},{64,80},{80,96},{96,112},{112,0},{1... | collective-permute-start | bytes 663560 | tf_op jit(solution)/shard_map/ppermute | solution.py:856
  8.7 0.9 fusion.4
  9.6 1.0 fusion.16
  11.8 1.2 fusion.1.g_ref.g5_ref
  14.3 2.1 %shard_map.69 = (f32[648,128]{1,0:T(8,128)}, f32[648,128]{1,0:T(8,128)}) custom-call(s32[4]{0:T(128)} %pad_add_fusion.4.ids_ref, f32[432,128]{1,0:T(8,128)} %get-tuple-element.35.lo_ref, f32[432,128]{1,0:T(8,128)} %get-tuple-element.36.hi_ref, f32[432,128]{1,0:T(8,128)} %copy-done.3, f32[432,128]{1,0:T(8,128)} %copy-done.4), custom_call_target="tpu_custom_call" | custom-call | tf_op jit(solution)/shard_map/pallas_call | solution.py:883
  16.4 1.6 collective-permute-start.2
  18.1 4.6 %collective-permute-start.3 = (f32[648,128]{1,0:T(8,128)}, f32[648,128]{1,0:T(8,128)S(1)}, u32[]{:S(2)}, u32[]{:S(2)}) collective-permute-start(f32[648,128]{1,0:T(8,128)} %get-tuple-element.38), channel_id=1, source_target_pairs={{0,15},{1,0},{2,1},{3,2},{4,3},{5,4},{6,5},{7,6},{8,7},{9,8},{10,9... | collective-permute-start | bytes 995336 | tf_op jit(solution)/shard_map/ppermute | solution.py:857
  22.7 6.8 %collective-permute-done.2.low_ref = f32[648,128]{1,0:T(8,128)S(1)} collective-permute-done((f32[648,128]{1,0:T(8,128)}, f32[648,128]{1,0:T(8,128)S(1)}, u32[]{:S(2)}, u32[]{:S(2)}) %collective-permute-start.2) | collective-permute-done | bytes 331808 | tf_op jit(solution)/shard_map/ppermute | solution.py:856
  30.4 12.9 %shard_map.70 = (f32[3456,128]{1,0:T(8,128)}, f32[3456,128]{1,0:T(8,128)}, f32[432,128]{1,0:T(8,128)}, f32[432,128]{1,0:T(8,128)}, f32[1024,128]{1,0:T(8,128)}, ...) custom-call(s32[4]{0:T(128)} %pad_add_fusion.4.ids_ref, ...), custom_call_target="tpu_custom_call" | custom-call | tf_op jit(solution)/shard_map/pallas_call | solution.py:887
  43.3 3.2 %collective-permute-start.4 = (f32[128,128]{1,0:T(8,128)}, f32[128,128]{1,0:T(8,128)S(1)}, u32[]{:S(2)}, u32[]{:S(2)}) collective-permute-start(f32[128,128]{1,0:T(8,128)} %get-tuple-element.41), channel_id=1, source_target_pairs={{0,16},{16,32},{32,48},{48,64},{64,80},{80,96},{96,112},{112,0},{1... | collective-permute-start | bytes 196616 | tf_op jit(solution)/shard_map/ppermute | solution.py:856
  46.6 1.6 collective-permute-done.4.left_ref
  48.2 2.3 %collective-permute-done.5.right_ref = f32[128,128]{1,0:T(8,128)S(1)} collective-permute-done((f32[128,128]{1,0:T(8,128)}, f32[128,128]{1,0:T(8,128)S(1)}, u32[]{:S(2)}, u32[]{:S(2)}) %collective-permute-start.5) | collective-permute-done | bytes 65568 | tf_op jit(solution)/shard_map/ppermute | solution.py:857
  51.0 1.6 shard_map.71
  52.6 4.8 %collective-permute-start.7 = (f32[192,128]{1,0:T(8,128)}, f32[192,128]{1,0:T(8,128)S(1)}, u32[]{:S(2)}, u32[]{:S(2)}) collective-permute-start(f32[192,128]{1,0:T(8,128)} %get-tuple-element.46), channel_id=1, source_target_pairs={{0,15},{1,0},{2,1},{3,2},{4,3},{5,4},{6,5},{7,6},{8,7},{9,8},{10,9... | collective-permute-start | bytes 294920 | tf_op jit(solution)/shard_map/ppermute | solution.py:857
  57.6 2.8 %collective-permute-done.6.low_ref = f32[192,128]{1,0:T(8,128)S(1)} collective-permute-done((f32[192,128]{1,0:T(8,128)}, f32[192,128]{1,0:T(8,128)S(1)}, u32[]{:S(2)}, u32[]{:S(2)}) %collective-permute-start.6) | collective-permute-done | bytes 98336 | tf_op jit(solution)/shard_map/ppermute | solution.py:856
  61.1 5.8 %shard_map.72 = (f32[1024,128]{1,0:T(8,128)}, f32[1024,128]{1,0:T(8,128)}, f32[1072,128]{1,0:T(8,128)}, f32[1072,128]{1,0:T(8,128)}, f32[16,128]{1,0:T(8,128)}) custom-call(s32[4]{0:T(128)} %pad_add_fusion.4.ids_ref, f32[1024,128]{1,0:T(8,128)} %get-tuple-element.39.s_ref, f32[1024,128]{1,0:T(8,128)} %get-tuple-element.40.bp_ref, f32[128,128]{1,0:T(8,128)} %copy-done.8, ...), custom_call_target="tpu_custom_call" | custom-call | tf_op jit(solution)/shard_map/pallas_call | solution.py:899
  66.9 1.2 collective-permute-start.8
  69.0 5.9 %collective-permute-done.8.left_ref = f32[1072,128]{1,0:T(8,128)S(1)} collective-permute-done((f32[1072,128]{1,0:T(8,128)}, f32[1072,128]{1,0:T(8,128)S(1)}, u32[]{:S(2)}, u32[]{:S(2)}) %collective-permute-start.8) | collective-permute-done | bytes 548896 | tf_op jit(solution)/shard_map/ppermute | solution.py:856
  74.8 2.7 %collective-permute-done.9.right_ref = f32[1072,128]{1,0:T(8,128)S(1)} collective-permute-done((f32[1072,128]{1,0:T(8,128)}, f32[1072,128]{1,0:T(8,128)S(1)}, u32[]{:S(2)}, u32[]{:S(2)}) %collective-permute-start.9) | collective-permute-done | bytes 548896 | tf_op jit(solution)/shard_map/ppermute | solution.py:857
  77.5 0.8 copy-done.2
  78.3 3.7 %shard_map.74 = (f32[2120,128]{1,0:T(8,128)}, f32[2120,128]{1,0:T(8,128)}) custom-call(s32[4]{0:T(128)} %pad_add_fusion.4.ids_ref, f32[3456,128]{1,0:T(8,128)} %get-tuple-element.51.r5_ref.r5p_ref, f32[1024,128]{1,0:T(8,128)} %get-tuple-element.53.r3_ref.r3p_ref, f32[1024,128]{1,0:T(8,128)} %get-tuple-element.54.z3_ref.z3p_ref, f32[1072,128]{1,0:T(8,128)} %copy-done.1, ...), custom_call_target="tpu_custom_call" | custom-call | tf_op jit(solution)/shard_map/pallas_call | solution.py:908
  82.0 5.0 %collective-permute-start.11 = (f32[2120,128]{1,0:T(8,128)}, f32[2120,128]{1,0:T(8,128)}, u32[]{:S(2)}, u32[]{:S(2)}) collective-permute-start(f32[2120,128]{1,0:T(8,128)} %get-tuple-element.58), channel_id=1, source_target_pairs={{0,15},{1,0},{2,1},{3,2},{4,3},{5,4},{6,5},{7,6},{8,7},{9,8},{10,9... | collective-permute-start | bytes 3256328 | tf_op jit(solution)/shard_map/ppermute | solution.py:857
  87.0 1.1 broadcast_in_dim.114
  88.1 5.4 %all-to-all-start = ((f32[128,16,128]{2,1,0:T(8,128)}), f32[128,16,128]{2,1,0:T(8,128)S(1)}, u32[]{:S(2)}, u32[]{:S(2)}) async-start(f32[128,16,128]{2,1,0:T(8,128)} %broadcast_in_dim.114), calls=%async_computation | async-start | bytes 2097152 | tf_op jit(solution)/shard_map/all_to_all | solution.py:906
  93.9 1.7 %broadcast_in_dim.115 = s32[17,72,2,64]{3,2,1,0:T(2,128)S(1)} broadcast(s32[17,72,2]{2,1,0:T(8,128)S(1)} %pad.38.clone), dimensions={0,1,2} | broadcast | bytes 636480 | tf_op jit(solution)/shard_map/broadcast_in_dim | solution.py:817
  96.9 2.2 %fusion.g3_ref = f32[3456,128]{1,0:T(8,128)} fusion(f32[2,128]{1,0:T(2,128)S(1)} %stack.153, f32[3456]{0:T(1024)S(1)} %mul.161, s32[3456]{0:T(1024)S(1)} %ge.82, s32[2,128]{1,0:T(2,128)S(1)} %copy-done.14), kind=kLoop, calls=%fused_computation.1 | loop fusion | flops 1327104 | bytes 1799168 | tf_op jit(solution)/shard_map/jit(_where)/select_n | solution.py:801
  99.2 1.1 multiply_select_fusion.w_ref
  100.2 23.5 %all-to-all-done = f32[128,16,128]{2,1,0:T(8,128)S(1)} async-done(((f32[128,16,128]{2,1,0:T(8,128)}), f32[128,16,128]{2,1,0:T(8,128)S(1)}, u32[]{:S(2)}, u32[]{:S(2)}) %all-to-all-start) | async-done | bytes 1048608 | tf_op jit(solution)/shard_map/all_to_all | solution.py:906
  123.8 1.0 copy-done
  124.8 11.6 %shard_map.73 = (f32[13,24,128]{2,1,0:T(8,128)}, f32[64,128]{1,0:T(8,128)}) custom-call(s32[4]{0:T(128)} %pad_add_fusion.4.ids_ref, f32[2048,128]{1,0:T(8,128)} %bitcast.71, f32[17,72,128]{2,1,0:T(8,128)} %multiply_select_fusion.w_ref, bf16[128,128]{1,0:T(8,128)(2,1)} %constant.90.clone.perm_ref), custom_call_target="tpu_custom_call" | custom-call | tf_op jit(solution)/shard_map/pallas_call | solution.py:912
  136.4 27.6 %shard_map.75 = f32[576,384]{1,0:T(8,128)} custom-call(s32[4]{0:T(128)} %pad_add_fusion.4.ids_ref, f32[13,24,128]{2,1,0:T(8,128)} %get-tuple-element.50.win_ref, f32[3456,128]{1,0:T(8,128)} %get-tuple-element.51.r5_ref.r5p_ref, f32[3456,128]{1,0:T(8,128)} %get-tuple-element.52.z5_ref, f32[1024,128]{1,0:T(8,128)} %get-tuple-element.53.r3_ref.r3p_ref, ...), custom_call_target="tpu_custom_call" | custom-call | tf_op jit(solution)/shard_map/pallas_call | solution.py:922
  (93 shorter events, 8.1 us)
Async XLA Ops:
  0.6 10.4 %copy-start.10 = (s32[32,64]{1,0:T(8,128)S(1)}, s32[32,64]{1,0:T(8,128)}, u32[]{:S(2)}) copy-start(s32[32,64]{1,0:T(8,128)} %param.6) | copy-start | bytes 24580
  5.4 7.6 %collective-permute-start = (f32[432,128]{1,0:T(8,128)}, f32[432,128]{1,0:T(8,128)S(1)}, u32[]{:S(2)}, u32[]{:S(2)}) collective-permute-start(f32[432,128]{1,0:T(8,128)} %get-tuple-element.33), channel_id=1, source_target_pairs={{0,16},{16,32},{32,48},{48,64},{64,80},{80,96},{96,112},{112,0},{1... | collective-permute-start | bytes 663560 | tf_op jit(solution)/shard_map/ppermute | solution.py:856
  8.0 5.6 %collective-permute-start.1 = (f32[432,128]{1,0:T(8,128)}, f32[432,128]{1,0:T(8,128)S(1)}, u32[]{:S(2)}, u32[]{:S(2)}) collective-permute-start(f32[432,128]{1,0:T(8,128)} %get-tuple-element.34), channel_id=1, source_target_pairs={{0,112},{16,0},{32,16},{48,32},{64,48},{80,64},{96,80},{112,96},{1... | collective-permute-start | bytes 663560 | tf_op jit(solution)/shard_map/ppermute | solution.py:857
  11.0 11.7 %copy-start.13 = (s32[2,128]{1,0:T(2,128)}, s32[2,128]{1,0:T(2,128)S(1)}, u32[]{:S(2)}) copy-start(s32[2,128]{1,0:T(2,128)S(1)} %pad_add_fusion.3) | copy-start | bytes 3076
  13.1 0.7 copy-start.3
  13.6 0.7 copy-start.4
  16.4 13.1 %collective-permute-start.2 = (f32[648,128]{1,0:T(8,128)}, f32[648,128]{1,0:T(8,128)S(1)}, u32[]{:S(2)}, u32[]{:S(2)}) collective-permute-start(f32[648,128]{1,0:T(8,128)} %get-tuple-element.37), channel_id=1, source_target_pairs={{0,1},{1,2},{2,3},{3,4},{4,5},{5,6},{6,7},{7,8},{8,9},{9,10},{10,1... | collective-permute-start | bytes 995336 | tf_op jit(solution)/shard_map/ppermute | solution.py:856
  18.1 11.5 %collective-permute-start.3 = (f32[648,128]{1,0:T(8,128)}, f32[648,128]{1,0:T(8,128)S(1)}, u32[]{:S(2)}, u32[]{:S(2)}) collective-permute-start(f32[648,128]{1,0:T(8,128)} %get-tuple-element.38), channel_id=1, source_target_pairs={{0,15},{1,0},{2,1},{3,2},{4,3},{5,4},{6,5},{7,6},{8,7},{9,8},{10,9... | collective-permute-start | bytes 995336 | tf_op jit(solution)/shard_map/ppermute | solution.py:857
  29.6 0.7 copy-start.5
  29.6 0.8 copy-start.6
  43.3 4.8 %collective-permute-start.4 = (f32[128,128]{1,0:T(8,128)}, f32[128,128]{1,0:T(8,128)S(1)}, u32[]{:S(2)}, u32[]{:S(2)}) collective-permute-start(f32[128,128]{1,0:T(8,128)} %get-tuple-element.41), channel_id=1, source_target_pairs={{0,16},{16,32},{32,48},{48,64},{64,80},{80,96},{96,112},{112,0},{1... | collective-permute-start | bytes 196616 | tf_op jit(solution)/shard_map/ppermute | solution.py:856
  46.5 3.9 %collective-permute-start.5 = (f32[128,128]{1,0:T(8,128)}, f32[128,128]{1,0:T(8,128)S(1)}, u32[]{:S(2)}, u32[]{:S(2)}) collective-permute-start(f32[128,128]{1,0:T(8,128)} %get-tuple-element.42), channel_id=1, source_target_pairs={{0,112},{16,0},{32,16},{48,32},{64,48},{80,64},{96,80},{112,96},{1... | collective-permute-start | bytes 196616 | tf_op jit(solution)/shard_map/ppermute | solution.py:857
  48.2 2.3 %copy-start.8 = (f32[128,128]{1,0:T(8,128)}, f32[128,128]{1,0:T(8,128)S(1)}, u32[]{:S(2)}) copy-start(f32[128,128]{1,0:T(8,128)S(1)} %collective-permute-done.4.left_ref) | copy-start | bytes 196612
  50.4 0.6 copy-start.9
  52.6 7.8 %collective-permute-start.6 = (f32[192,128]{1,0:T(8,128)}, f32[192,128]{1,0:T(8,128)S(1)}, u32[]{:S(2)}, u32[]{:S(2)}) collective-permute-start(f32[192,128]{1,0:T(8,128)} %get-tuple-element.45), channel_id=1, source_target_pairs={{0,1},{1,2},{2,3},{3,4},{4,5},{5,6},{6,7},{7,8},{8,9},{9,10},{10,1... | collective-permute-start | bytes 294920 | tf_op jit(solution)/shard_map/ppermute | solution.py:856
  52.6 7.8 %collective-permute-start.7 = (f32[192,128]{1,0:T(8,128)}, f32[192,128]{1,0:T(8,128)S(1)}, u32[]{:S(2)}, u32[]{:S(2)}) collective-permute-start(f32[192,128]{1,0:T(8,128)} %get-tuple-element.46), channel_id=1, source_target_pairs={{0,15},{1,0},{2,1},{3,2},{4,3},{5,4},{6,5},{7,6},{8,7},{9,8},{10,9... | collective-permute-start | bytes 294920 | tf_op jit(solution)/shard_map/ppermute | solution.py:857
  60.4 0.6 copy-start.11
  60.4 0.7 copy-start.12
  66.9 7.9 %collective-permute-start.8 = (f32[1072,128]{1,0:T(8,128)}, f32[1072,128]{1,0:T(8,128)S(1)}, u32[]{:S(2)}, u32[]{:S(2)}) collective-permute-start(f32[1072,128]{1,0:T(8,128)} %get-tuple-element.55), channel_id=1, source_target_pairs={{0,16},{16,32},{32,48},{48,64},{64,80},{80,96},{96,112},{112,0},{1... | collective-permute-start | bytes 1646600 | tf_op jit(solution)/shard_map/ppermute | solution.py:856
  68.1 9.4 %collective-permute-start.9 = (f32[1072,128]{1,0:T(8,128)}, f32[1072,128]{1,0:T(8,128)S(1)}, u32[]{:S(2)}, u32[]{:S(2)}) collective-permute-start(f32[1072,128]{1,0:T(8,128)} %get-tuple-element.56), channel_id=1, source_target_pairs={{0,112},{16,0},{32,16},{48,32},{64,48},{80,64},{96,80},{112,96},{1... | collective-permute-start | bytes 1646600 | tf_op jit(solution)/shard_map/ppermute | solution.py:857
  74.8 2.7 %copy-start.1 = (f32[1072,128]{1,0:T(8,128)}, f32[1072,128]{1,0:T(8,128)S(1)}, u32[]{:S(2)}) copy-start(f32[1072,128]{1,0:T(8,128)S(1)} %collective-permute-done.8.left_ref) | copy-start | bytes 1646596
  77.5 0.8 copy-start.2
  78.3 8.7 %copy-start.15 = (f32[16,128]{1,0:T(8,128)S(1)}, f32[16,128]{1,0:T(8,128)}, u32[]{:S(2)}) copy-start(f32[16,128]{1,0:T(8,128)} %get-tuple-element.49) | copy-start | bytes 24580
  82.0 54.4 %collective-permute-start.10 = (f32[2120,128]{1,0:T(8,128)}, f32[2120,128]{1,0:T(8,128)}, u32[]{:S(2)}, u32[]{:S(2)}) collective-permute-start(f32[2120,128]{1,0:T(8,128)} %get-tuple-element.57), channel_id=1, source_target_pairs={{0,1},{1,2},{2,3},{3,4},{4,5},{5,6},{6,7},{7,8},{8,9},{9,10},{10,1... | collective-permute-start | bytes 3256328 | tf_op jit(solution)/shard_map/ppermute | solution.py:856
  82.0 54.4 %collective-permute-start.11 = (f32[2120,128]{1,0:T(8,128)}, f32[2120,128]{1,0:T(8,128)}, u32[]{:S(2)}, u32[]{:S(2)}) collective-permute-start(f32[2120,128]{1,0:T(8,128)} %get-tuple-element.58), channel_id=1, source_target_pairs={{0,15},{1,0},{2,1},{3,2},{4,3},{5,4},{6,5},{7,6},{8,7},{9,8},{10,9... | collective-permute-start | bytes 3256328 | tf_op jit(solution)/shard_map/ppermute | solution.py:857
  88.1 35.7 %all-to-all-start = ((f32[128,16,128]{2,1,0:T(8,128)}), f32[128,16,128]{2,1,0:T(8,128)S(1)}, u32[]{:S(2)}, u32[]{:S(2)}) async-start(f32[128,16,128]{2,1,0:T(8,128)} %broadcast_in_dim.114), calls=%async_computation | async-start | bytes 2097152 | tf_op jit(solution)/shard_map/all_to_all | solution.py:906
  93.9 2.5 %copy-start.7 = (f32[12,3,3,12]{3,2,1,0:T(4,128)S(1)}, f32[12,3,3,12]{3,2,1,0:T(4,128)}, u32[]{:S(2)}) copy-start(f32[12,3,3,12]{3,2,1,0:T(4,128)} %broadcast_multiply_fusion) | copy-start | bytes 15556
  95.6 1.2 copy-start.14
  123.8 1.0 copy-start

commit v2 on v1

--- a/solution.py
+++ b/solution.py
@@ -10,6 +10,7 @@
 
 CG_ITERS = 10
 VMEM = pl.BlockSpec(memory_space=pltpu.VMEM)
+ANY = pl.BlockSpec(memory_space=pl.ANY)
 SMEM = pl.BlockSpec(memory_space=pltpu.SMEM)
 F32 = jnp.float32
 
@@ -166,6 +167,24 @@
         emit(i, t)
 
 
+def k_face(n, src, a_src, i, rows, emit):
+    s, w = lagrange_tables(n)
+    sh = s / w[:, None]
+    kh, cnt = n // 2, per(n)
+    base = a_src * cnt
+    v = [[ld(src, base + ix(n, i, j, k), rows) for k in range(kh)] for j in range(n)]
+    t = [cs_fold(sh, v[j]) for j in range(n)]
+    for k in range(kh):
+        line = cs_apply(sh, [v[j][k] for j in range(n)])
+        for j in range(n):
+            total = t[j][k] + line[j]
+            for q in range(n):
+                x = v[j][k] if q == i else ld(src, base + ix(n, q, j, k), rows)
+                total = total + x * float(sh[i, q])
+            t[j][k] = total * float(w[i] * w[j] * w[k])
+    emit(i, t)
+
+
 def z_partner(v):
     lane = lane_iota(v.shape[0])
     moved = jnp.where(lane < 64, pltpu.roll(v, 65, 1), pltpu.roll(v, 63, 1))
@@ -187,6 +206,20 @@
     for j in range(n):
         for k in range(n // 2):
             st(ref, base + ix(n, i, j, k), rows, t[j][k])
+
+
+def apply_columns(n, src, t_ref, acc_ref, lo, hi, rows):
+    def put(a):
+        return lambda i, t: put_plane(n, t_ref, a * per(n), i, zy_sum(n, t), rows)
+
+    k_face(n, src, lo, n - 1, rows, put(lo))
+    k_face(n, src, hi - 1, 0, rows, put(hi - 1))
+
+    def body(a, carry):
+        k_slab(n, src, a, acc_ref, rows, put(a))
+        return carry
+
+    lax.fori_loop(lo + 1, hi - 1, body, 0)
 
 
 def x_summed(n, ref, a, i, j, k, rows, low=True, high=True):
@@ -400,12 +433,7 @@
 
     lax.fori_loop(0, 6, first, 0)
 
-    def second(a, carry):
-        put = lambda i, t: put_plane(n, t_ref, a * cnt, i, zy_sum(n, t), 8)
-        k_slab(n, u_ref, a, acc_ref, 8, put)
-        return carry
-
-    lax.fori_loop(0, 6, second, 0)
+    apply_columns(n, u_ref, t_ref, acc_ref, 0, 6, 8)
 
     def third(a, carry):
         for i, j, k in nodes(n):
@@ -455,13 +483,18 @@
 
 
 def fine_down_kernel(
-    ids_ref, s_ref, bp_ref, left_ref, right_ref, low_ref, high_ref, g_ref,
-    z_ref, rp_ref, ml_ref, mr_ref, s3_ref, b3_ref, m3l_ref, m3r_ref, lo3_ref, hi3_ref,
-    b_ref, u_ref, t_ref, acc_ref, w1_ref, w2_ref, t3_ref,
+    ids_ref, s_in, bp_ref, left_ref, right_ref, low_ref, high_ref, g_ref,
+    z_out, rp_ref, ml_ref, mr_ref, lo_ref, hi_ref, s3_ref, b3_ref, m3l_ref, m3r_ref, lo3_ref, hi3_ref,
+    b_ref, u_ref, t_ref, acc_ref, w1_ref, w2_ref, t3_ref, s_ref, z_ref, sem,
 ):
     fl = flags(ids_ref)
+    get_s = pltpu.make_async_copy(s_in, s_ref, sem.at[0])
+    put_z = pltpu.make_async_copy(z_ref, z_out, sem.at[1])
+    get_s.start()
     unpack(6, 1, 1, 8, 2, bp_ref, left_ref, right_ref, low_ref, high_ref, (0, 0), fl, b_ref, True)
     down_smooth(6, b_ref, g_ref, 1, u_ref, t_ref, acc_ref, z_ref)
+    put_z.start()
+    get_s.wait()
     c3 = per(4)
     zero_face(4, t3_ref, 0, 3, 8)
     zero_face(4, t3_ref, 5, 0, 8)
@@ -479,15 +512,17 @@
     own_row_lines(4, b3_ref, lo3_ref, hi3_ref)
     pack_column(6, rp_ref, 0, ml_ref, 0)
     pack_column(6, rp_ref, 3, mr_ref, 0)
-
-
-X5, X3R, X3Z = 108 * 4, 3 * 32 * 4, 2 * 32 * 4
-Y5, Y3R, Y3Z = 6 * 108, 3 * 10 * 32, 2 * 8 * 32
+    own_row_lines(6, rp_ref, lo_ref, hi_ref)
+    put_z.wait()
+
+
+X3R, X3Z = 3 * 32 * 4, 2 * 32 * 4
+Y3R, Y3Z = 3 * 10 * 32, 2 * 8 * 32
 
 
 def middle_down_kernel(
-    ids_ref, s_ref, bp_ref, left_ref, right_ref, low_ref, high_ref, g_ref, m5l_ref, m5r_ref,
-    z_ref, rp_ref, ml_ref, mr_ref, block_ref,
+    ids_ref, s_ref, bp_ref, left_ref, right_ref, low_ref, high_ref, g_ref,
+    z_ref, rp_ref, block_ref, ml_ref, mr_ref,
     b_ref, u_ref, t_ref, acc_ref, w1_ref, w2_ref, c_ref,
 ):
     fl = flags(ids_ref)
@@ -515,27 +550,30 @@
             v = u if v is None else v + u
         planes.append(v)
     lane = lane_iota()
-    block_ref[...] = jnp.zeros((16, 128), F32)
+    blank = jnp.zeros((1, 128), F32)
+    rows = []
     for p in range(3):
         v = planes[2 * p]
         other = swap(planes[2 * p + 1]) if p < 2 else jnp.zeros((8, 128), F32)
         v = jnp.where(lane < 64, v, other)
-        block_ref[pl.ds(5 * p, 5), :] = v[2:7]
-    ml_ref[pl.ds(0, X5), :] = m5l_ref[...]
-    mr_ref[pl.ds(0, X5), :] = m5r_ref[...]
+        rows.append(v[2:7])
+    block = jnp.concatenate(rows + [blank], axis=0)
+    for d in range(block_ref.shape[0] // 16):
+        block_ref[pl.ds(16 * d, 16), :] = block
+
     for t in range(3):
-        pack_column(4, rp_ref, t, ml_ref, X5 // 8 + t * 16)
-        pack_column(4, rp_ref, 1 + t, mr_ref, X5 // 8 + t * 16)
+        pack_column(4, rp_ref, t, ml_ref, t * 16)
+        pack_column(4, rp_ref, 1 + t, mr_ref, t * 16)
     for t in range(2):
-        pack_column(4, z_ref, t, ml_ref, (X5 + X3R) // 8 + t * 16)
-        pack_column(4, z_ref, 2 + t, mr_ref, (X5 + X3R) // 8 + t * 16)
-
-
-def up_lines_kernel(ids_ref, r5_ref, r3_ref, z3_ref, left_ref, right_ref, dn_ref, up_ref):
+        pack_column(4, z_ref, t, ml_ref, X3R // 8 + t * 16)
+        pack_column(4, z_ref, 2 + t, mr_ref, X3R // 8 + t * 16)
+
+
+def up_lines_kernel(ids_ref, r3_ref, z3_ref, left_ref, right_ref, dn_ref, up_ref):
     fl, fr, _, _ = flags(ids_ref)
-    for dst, r5row, r3rows, z3rows in (
-        (dn_ref, 0, (0, 1, 2), (0, 1)),
-        (up_ref, 3, (1, 2, 3), (2, 3)),
+    for dst, r3rows, z3rows in (
+        (dn_ref, (0, 1, 2), (0, 1)),
+        (up_ref, (1, 2, 3), (2, 3)),
     ):
         def line(src, cnt, b):
             return lambda a: src[pl.ds(a * cnt * 8 + 2 + b, cnt, stride=8), :]
@@ -543,24 +581,20 @@
         def part(ref, start, size):
             return ref.at[pl.ds(start, size), :]
 
-        y_line(
-            6, 1, line(r5_ref, 108, r5row), fl, fr, part(left_ref, 0, X5), part(right_ref, 0, X5),
-            r5row, dst, 0, True,
-        )
         for t, b in enumerate(r3rows):
             y_line(
-                4, 3, line(r3_ref, 32, b), fl, fr, part(left_ref, X5, X3R),
-                part(right_ref, X5, X3R), b, dst, Y5 + t * 320, True,
+                4, 3, line(r3_ref, 32, b), fl, fr, part(left_ref, 0, X3R),
+                part(right_ref, 0, X3R), b, dst, t * 320, True,
             )
         for t, b in enumerate(z3rows):
             y_line(
-                4, 2, line(z3_ref, 32, b), fl, fr, part(left_ref, X5 + X3R, X3Z),
-                part(right_ref, X5 + X3R, X3Z), b, dst, Y5 + Y3R + t * 256, False,
+                4, 2, line(z3_ref, 32, b), fl, fr, part(left_ref, X3R, X3Z),
+                part(right_ref, X3R, X3Z), b, dst, Y3R + t * 256, False,
             )
 
 
 def coarse_kernel(
-    ids_ref, gath_ref, w_ref, perm_ref, win_ref, out_ref, x_ref, r_ref, p_ref, q_ref, o_ref
+    ids_ref, same_ref, other_ref, w_ref, perm_ref, win_ref, out_ref, x_ref, r_ref, p_ref, q_ref, o_ref
 ):
     gy = ids_ref[1]
     gx = ids_ref[0]
@@ -569,13 +603,18 @@
     for ref in (x_ref, r_ref, p_ref, q_ref):
         ref[...] = jnp.zeros(ref.shape, F32)
     lane16 = lane_iota(16)
+    even = lax.rem(gx, 2) == 0
+
+    def lines(g, row):
+        where = pl.ds((g // 2) * 256 + row, 16, stride=16)
+        u, v = same_ref[where, :], other_ref[where, :]
+        return jnp.where(even, u, v) if g % 2 == 0 else jnp.where(even, v, u)
+
     for g in range(4):
         for i in range(5):
             for r in range(5):
-                lo = gath_ref[pl.ds((g * 16) * 16 + (i // 2) * 5 + r, 16, stride=16), :]
-                hi = gath_ref[
-                    pl.ds(((7 - g) * 16) * 16 + ((4 - i) // 2) * 5 + r, 16, stride=16), :
-                ]
+                lo = lines(g, (i // 2) * 5 + r)
+                hi = lines(7 - g, ((4 - i) // 2) * 5 + r)
                 if i % 2 == 0:
                     v = jnp.where(lane16 < 64, lo, swap(hi))
                 else:
@@ -649,20 +688,13 @@
     out_ref[...] = exact_dot(o_ref[...], perm_ref[...])
 
 
-def up_smooth(n, wide, rows, v_ref, r_ref, g_ref, u_ref, t_ref, acc_ref, finish):
+def up_smooth(n, wide, rows, v_ref, r_ref, g_ref, u_ref, t_ref, acc_ref, before_residual, finish):
     center, ca, cb = cheb(n)
     d = diag_table(n)
     cnt = per(n)
 
-    def apply_to(src, lo, hi):
-        def body(a, carry):
-            put = lambda i, t: put_plane(n, t_ref, a * cnt, i, zy_sum(n, t), rows)
-            k_slab(n, src, a, acc_ref, rows, put)
-            return carry
-
-        lax.fori_loop(lo, hi, body, 0)
-
-    apply_to(v_ref, 0, wide)
+    apply_columns(n, v_ref, t_ref, acc_ref, 0, wide, rows)
+    before_residual()
 
     def first(a, carry):
         for i, j, k in nodes(n):
@@ -674,7 +706,7 @@
         return carry
 
     lax.fori_loop(1, wide - 1, first, 0)
-    apply_to(u_ref, 1, wide - 1)
+    apply_columns(n, u_ref, t_ref, acc_ref, 1, wide - 1, rows)
 
     def second(a, carry):
         for i, j, k in nodes(n):
@@ -689,24 +721,42 @@
 
 
 def up_kernel(
-    ids_ref, win_ref, r5p_ref, z5_ref, r3p_ref, z3p_ref, left_ref, right_ref, low_ref, high_ref,
-    g5_ref, g3_ref, perm_ref, out_ref,
+    ids_ref, win_ref, r5p_in, z5_in, r3p_in, z3p_in, left_in, right_in, low_in, high_in,
+    left5_in, right5_in, low5_in, high5_in,
+    g5_in, g3_in, perm_ref, out_ref,
+    r5p_ref, z5_ref, r3p_ref, z3p_ref, left_ref, right_ref, low_ref, high_ref,
+    left5_ref, right5_ref, low5_ref, high5_ref, g5_ref, g3_ref, sem,
     v3_ref, r3_ref, z3_ref, u3_ref, t3_ref, a3_ref, v5_ref, r5_ref, u5_ref, t5_ref, a5_ref,
     w1_ref, w2_ref, y_ref,
 ):
     fl = flags(ids_ref)
     c3, c5 = per(4), per(6)
-
-    def take(n, h, a0, rows, r0, own, offs, dst, partial):
-        unpack(
-            n, h, a0, rows, r0, own, left_ref, right_ref, low_ref, high_ref, offs, fl, dst, partial
-        )
-
-    take(6, 1, 2, 8, 2, r5p_ref, (0, 0), r5_ref, True)
-    take(4, 3, 4, 16, 4, r3p_ref, (X5, Y5), r3_ref, True)
-    take(4, 2, 4, 16, 4, z3p_ref, (X5 + X3R, Y5 + Y3R), z3_ref, False)
+    moves = [
+        (g3_in, g3_ref), (left_in, left_ref), (right_in, right_ref), (low_in, low_ref),
+        (high_in, high_ref), (r3p_in, r3p_ref), (z3p_in, z3p_ref), (r5p_in, r5p_ref),
+        (left5_in, left5_ref), (right5_in, right5_ref), (low5_in, low5_ref),
+        (high5_in, high5_ref), (g5_in, g5_ref), (z5_in, z5_ref),
+    ]
+    moves = [pltpu.make_async_copy(a, b, sem.at[m]) for m, (a, b) in enumerate(moves)]
+    for move in moves:
+        move.start()
+
+    def take3():
+        for move in moves[1:7]:
+            move.wait()
+        refs = (left_ref, right_ref, low_ref, high_ref)
+        unpack(4, 3, 4, 16, 4, r3p_ref, *refs, (0, 0), fl, r3_ref, True)
+        unpack(4, 2, 4, 16, 4, z3p_ref, *refs, (X3R, Y3R), fl, z3_ref, False)
+
+    def take5():
+        for move in moves[7:12]:
+            move.wait()
+        refs = (left5_ref, right5_ref, low5_ref, high5_ref)
+        unpack(6, 1, 2, 8, 2, r5p_ref, *refs, (0, 0), fl, r5_ref, True)
+        moves[13].wait()
 
     m = interpolation(2, 4)
+    moves[0].wait()
 
     def prolong1(a, carry):
         corner = [[[win_ref[a + i, pl.ds(j, 16), :]] for j in range(2)] for i in range(2)]
@@ -726,9 +776,10 @@
         s = a * c3 + ix(4, i, j, k)
         st(z3_ref, s, 16, ld(z3_ref, s, 16) + x)
 
-    up_smooth(4, 12, 16, v3_ref, r3_ref, g3_ref, u3_ref, t3_ref, a3_ref, finish3)
+    up_smooth(4, 12, 16, v3_ref, r3_ref, g3_ref, u3_ref, t3_ref, a3_ref, take3, finish3)
 
     m5 = interpolation(4, 6)
+    moves[12].wait()
 
     def prolong3(a, carry):
         for j in range(4):
@@ -759,7 +810,7 @@
         start = ((a - 2) * 6 + i) * 24 + j
         y_ref[pl.ds(576 * k + start, 4, stride=6), :] = v[2:6]
 
-    up_smooth(6, 8, 8, v5_ref, r5_ref, g5_ref, u5_ref, t5_ref, a5_ref, finish5)
+    up_smooth(6, 8, 8, v5_ref, r5_ref, g5_ref, u5_ref, t5_ref, a5_ref, take5, finish5)
     y = jnp.concatenate([y_ref[pl.ds(576 * k, 576), :] for k in range(3)], axis=1)
     out_ref[...] = exact_dot(y, perm_ref[...])
 
@@ -840,13 +891,13 @@
     return m
 
 
-def call(kernel, outs, ins, scratch):
+def call(kernel, outs, ins, scratch, out_specs=None):
     return pl.pallas_call(
         kernel,
         out_shape=[jax.ShapeDtypeStruct(s, F32) for s in outs],
         in_specs=ins,
-        out_specs=[VMEM] * len(outs),
-        scratch_shapes=[pltpu.VMEM(s, F32) for s in scratch],
+        out_specs=out_specs or [VMEM] * len(outs),
+        scratch_shapes=[pltpu.VMEM(s, F32) if isinstance(s, tuple) else s for s in scratch],
         compiler_params=pltpu.CompilerParams(vmem_limit_bytes=56 * 1024 * 1024),
     )
 
@@ -864,8 +915,6 @@
     ids = jnp.stack([gx, gy, nx, ny]).astype(jnp.int32)
     g5 = class_maps(heights, gx, gy, 2, 8, 2)
     g3d = class_maps(heights, gx, gy, 2, 8, 2)
-    g3 = class_maps(heights, gx, gy, 4, 16, 4)
-    cw = coarse_weight(heights)
     pin = jnp.asarray(perm_in(), jnp.bfloat16)
     pout = jnp.asarray(perm_in().T, jnp.bfloat16)
     pc = jnp.asarray(perm_coarse(), jnp.bfloat16)
@@ -880,41 +929,58 @@
         [(1872, 128), f(6, 6)],
     )(source.reshape(576, 384), pin)
     left, right = both_ways("gx", ml, mr)
+    left, later = lax.optimization_barrier((left, heights))
+    g3 = class_maps(later, gx, gy, 4, 16, 4)
+    cw = coarse_weight(later)
     dn, up = call(
         functools.partial(y_lines_kernel, 6), [(648, 128)] * 2, [SMEM] + [VMEM] * 4, []
     )(ids, lo, hi, left, right)
     low, high = both_ways("gy", dn, up)
-    z5, r5p, m5l, m5r, s3, b3p, ml, mr, lo, hi = call(
+    low, g3, cw = lax.optimization_barrier((low, g3, cw))
+    z5, r5p, m5l, m5r, lo5, hi5, s3, b3p, ml, mr, lo, hi = call(
         fine_down_kernel,
-        [f(6, 4), f(6, 4), (432, 128), (432, 128), f(4, 4), f(4, 4)] + [(128, 128)] * 4,
-        [SMEM] + [VMEM] * 7,
-        [f(6, 6), f(6, 6), f(6, 6), f(6, 1), f(6, 1), f(6, 1), f(4, 6)],
+        [f(6, 4), f(6, 4)] + [(432, 128)] * 4 + [f(4, 4), f(4, 4)] + [(128, 128)] * 4,
+        [SMEM, ANY] + [VMEM] * 6,
+        [f(6, 6), f(6, 6), f(6, 6), f(6, 1), f(6, 1), f(6, 1), f(4, 6), f(6, 4), f(6, 4)]
+        + [pltpu.SemaphoreType.DMA((2,))],
+        [ANY] + [VMEM] * 11,
     )(ids, s5, b5p, left, right, low, high, g5)
     left, right = both_ways("gx", ml, mr)
+    left5, right5 = both_ways("gx", m5l, m5r)
     dn, up = call(
         functools.partial(y_lines_kernel, 4), [(192, 128)] * 2, [SMEM] + [VMEM] * 4, []
     )(ids, lo, hi, left, right)
     low, high = both_ways("gy", dn, up)
-    xr, yr = X5 + X3R + X3Z, Y5 + Y3R + Y3Z
-    z3, r3p, ml, mr, block = call(
+    left5, dn = lax.optimization_barrier((left5, dn))
+    dn5, up5 = call(
+        functools.partial(y_lines_kernel, 6), [(648, 128)] * 2, [SMEM] + [VMEM] * 4, []
+    )(ids, lo5, hi5, left5, right5)
+    low, dn5, up5 = lax.optimization_barrier((low, dn5, up5))
+    low5, high5 = both_ways("gy", dn5, up5)
+    xr, yr = X3R + X3Z, Y3R + Y3Z
+    z3, r3p, block, ml, mr = call(
         middle_down_kernel,
-        [f(4, 4), f(4, 4), (xr, 128), (xr, 128), (16, 128)],
-        [SMEM] + [VMEM] * 9,
+        [f(4, 4), f(4, 4), (nx * ny * 8, 128), (xr, 128), (xr, 128)],
+        [SMEM] + [VMEM] * 7,
         [f(4, 6), f(4, 6), f(4, 6), f(4, 1), f(4, 1), f(4, 1), (64, 128)],
-    )(ids, s3, b3p, left, right, low, high, g3d, m5l, m5r)
-    every = jnp.broadcast_to(block[None], (nx * ny, 16, 128))
-    gath = lax.all_to_all(every, ("gx", "gy"), 0, 0).reshape(nx * ny * 16, 128)
+    )(ids, s3, b3p, left, right, low, high, g3d)
+    every = block.reshape(nx * ny // 2, 16, 128)
+    groups = [[(2 * x + c) * ny + y for x in range(nx // 2) for y in range(ny)] for c in range(2)]
+    same = lax.all_to_all(every, ("gx", "gy"), 0, 0, axis_index_groups=groups)
+    same = same.reshape(nx * ny * 8, 128)
+    other = lax.ppermute(same, "gx", [(i, i ^ 1) for i in range(nx)])
     left, right = both_ways("gx", ml, mr)
-    dn, up = call(up_lines_kernel, [(yr, 128)] * 2, [SMEM] + [VMEM] * 5, [])(
-        ids, r5p, r3p, z3, left, right
+    left, low5, high5 = lax.optimization_barrier((left, low5, high5))
+    dn, up = call(up_lines_kernel, [(yr, 128)] * 2, [SMEM] + [VMEM] * 4, [])(
+        ids, r3p, z3, left, right
     )
     low, high = both_ways("gy", dn, up)
     win, coarse = call(
         coarse_kernel,
         [(13, 24, 128), (64, 128)],
-        [SMEM] + [VMEM] * 3,
+        [SMEM] + [VMEM] * 4,
         [(17, 88, 128)] * 4 + [(64, 128)],
-    )(ids, gath, cw, pc)
+    )(ids, same, other, cw, pc)
 
     def f16(a):
         return (a * per(4) * 16, 128)
@@ -922,10 +988,14 @@
     (out,) = call(
         up_kernel,
         [(576, 384)],
-        [SMEM] + [VMEM] * 12,
-        [f16(12), f16(12), f16(12), f16(12), f16(12), f16(1)]
+        [SMEM, VMEM] + [ANY] * 14 + [VMEM],
+        [f(6, 4), f(6, 4), f(4, 4), f(4, 4), (xr, 128), (xr, 128), (yr, 128), (yr, 128)]
+        + [(432, 128), (432, 128), (648, 128), (648, 128)]
+        + [(8 * 18 * 8, 128), (12 * 18 * 16, 128), pltpu.SemaphoreType.DMA((14,)), f16(12), f16(12), f16(12), f16(12), f16(12), f16(1)]
         + [f(6, 8), f(6, 8), f(6, 8), f(6, 8), f(6, 1), f(6, 1), f(6, 1), (1728, 128)],
-    )(ids, win, r5p, z5, r3p, z3, left, right, low, high, g5, g3, pout)
+    )(
+        ids, win, r5p, z5, r3p, z3, left, right, low, high, left5, right5, low5, high5, g5, g3, pout
+    )
     return out.reshape(24, 24, 384), coarse.reshape(8, 8, 128)
 
 

time: 165 us -> 134 us (0.81)
  waiting for transfers between devices: 46 us -> 9.49 us
  starting transfers between devices: 28.4 us -> 39.5 us
  Pallas kernels: 70.2 us -> 66.1 us
    all_to_all x1, waiting for transfers between devices: 23.5 us -> 0.6 us  [per_device(): same = lax.all_to_all(every, ('gx', 'gy'), 0, 0, axis_index_groups=groups)]
    ppermute x6 -> x8, waiting for transfers between devices: 17 us -> 2.59 us  [both_ways(): from_low = lax.ppermute(to_high, axis, [(i, (i + 1) % n) for i in range(n)])]
    pallas_call x5, Pallas kernels: 61.6 us -> 55.4 us  [the longest x1 23.8 us: per_device(): call(up_kernel, [(576, 384)], [SMEM, VMEM] + [ANY] * 14 + [VMEM], [f(6, 4...]
    ppermute x6 -> x8, starting transfers between devices: 14.4 us -> 19.2 us  [both_ways(): from_high = lax.ppermute(to_low, axis, [(i, (i - 1) % n) for i in range(n)])]
    ppermute x0 -> x1, starting transfers between devices: none -> 4.52 us  [per_device(): other = lax.ppermute(same, 'gx', [(i, i ^ 1) for i in range(nx)])]
    ppermute x6 -> x8, starting transfers between devices: 8.63 us -> 10.9 us  [both_ways(): from_low = lax.ppermute(to_high, axis, [(i, (i + 1) % n) for i in range(n)])]
    pallas_call x1 -> x2, Pallas kernels: 2.14 us -> 4.29 us  [per_device(): call(functools.partial(y_lines_kernel, 6), [(648, 128)] * 2, [SMEM] + [VM...]
    unnamed x34 -> x40, local copies, waits for them, and re-layouts: 5.01 us -> 6.57 us
  transfers between devices with their start and end apart: 13 -> 18, of which waited for: 8 -> 7; matrix products, arithmetic and copies ran while one was open for 8% -> 8% of each run, Pallas kernels for 7% -> 18%
where the time goes in v2:
time: 134 us
  Pallas kernels  66.1 us (49%)
  starting transfers between devices  39.5 us (29%)
  local copies, waits for them, and re-layouts  10.1 us (8%)
  waiting for transfers between devices  9.49 us (7%)
  other arithmetic  7.34 us (5%)
    pallas_call x1, Pallas kernels, per_device(): call(up_kernel, [(576, 384)], [SMEM, VMEM] + [ANY] * 14 + [VMEM], [f(6, 4...  23.8 us
    ppermute x8, starting transfers between devices, both_ways(): from_high = lax.ppermute(to_low, axis, [(i, (i - 1) % n) for i in range(n)])  19.2 us
    pallas_call x1, Pallas kernels, per_device(): call(coarse_kernel, [(13, 24, 128), (64, 128)], [SMEM] + [VMEM] * 4, [(17...  12 us
    pallas_call x1, Pallas kernels, per_device(): call(fine_down_kernel, [f(6, 4), f(6, 4)] + [(432, 128)] * 4 + [f(4, 4),...  11.4 us
    ppermute x8, starting transfers between devices, both_ways(): from_low = lax.ppermute(to_high, axis, [(i, (i + 1) % n) for i in range(n)])  10.9 us
    unnamed x40, local copies, waits for them, and re-layouts  6.57 us
    pallas_call x1, Pallas kernels, per_device(): call(middle_down_kernel, [f(4, 4), f(4, 4), (nx * ny * 8, 128), (xr, 128)...  5.55 us
    all_to_all x1, starting transfers between devices, per_device(): same = lax.all_to_all(every, ('gx', 'gy'), 0, 0, axis_index_groups=groups)  4.84 us
  transfers between devices with their start and end apart: 18, of which 7 were waited for; matrix products, arithmetic and copies ran while one was open for 8% of the time, Pallas kernels for 18%

profile of v2, /device:TPU:1, one launch (start us, length us, event | category | flops | bytes accessed | tf_op | source)
XLA Modules:
  0.0 133.7 jit_solution(5669985453959382395)
XLA Ops:
  0.6 4.8 %shard_map.68 = (f32[3456,128]{1,0:T(8,128)}, f32[3456,128]{1,0:T(8,128)}, f32[432,128]{1,0:T(8,128)}, f32[432,128]{1,0:T(8,128)}, f32[432,128]{1,0:T(8,128)}, /*index=5*/f32[432,128]{1,0:T(8,128)}) custom-call(f32[576,384]{1,0:T(8,128)} %bitcast.74, bf16[384,384]{1,0:T(8,128)(2,1)} %constant.24.clone.perm_ref), custom_call_target="tpu_custom_call" | custom-call | tf_op jit(solution)/shard_map/pallas_call | solution.py:925
  5.5 2.6 %collective-permute-start = (f32[432,128]{1,0:T(8,128)}, f32[432,128]{1,0:T(8,128)S(1)}, u32[]{:S(2)}, u32[]{:S(2)}) collective-permute-start(f32[432,128]{1,0:T(8,128)} %get-tuple-element.49), channel_id=1, source_target_pairs={{0,16},{16,32},{32,48},{48,64},{64,80},{80,96},{96,112},{112,0},{1... | collective-permute-start | bytes 663560 | tf_op jit(solution)/shard_map/ppermute | solution.py:907
  8.8 1.0 fusion.16
  11.5 1.2 fusion.1.g_ref.g5_in
  14.3 2.1 %shard_map.69 = (f32[648,128]{1,0:T(8,128)}, f32[648,128]{1,0:T(8,128)}) custom-call(s32[4]{0:T(128)} %pad_add_fusion.4.ids_ref, f32[432,128]{1,0:T(8,128)} %get-tuple-element.52.lo_ref, f32[432,128]{1,0:T(8,128)} %get-tuple-element.53.hi_ref, f32[432,128]{1,0:T(8,128)} %copy-done.3, f32[432,128]{1,0:T(8,128)} %copy-done.4), custom_call_target="tpu_custom_call" | custom-call | tf_op jit(solution)/shard_map/pallas_call | solution.py:935
  16.5 1.6 %collective-permute-start.2 = (f32[648,128]{1,0:T(8,128)}, f32[648,128]{1,0:T(8,128)S(1)}, u32[]{:S(2)}, u32[]{:S(2)}) collective-permute-start(f32[648,128]{1,0:T(8,128)} %get-tuple-element.54), channel_id=1, source_target_pairs={{0,1},{1,2},{2,3},{3,4},{4,5},{5,6},{6,7},{7,8},{8,9},{9,10},{10,1... | collective-permute-start | bytes 995336 | tf_op jit(solution)/shard_map/ppermute | solution.py:907
  18.1 4.6 %collective-permute-start.3 = (f32[648,128]{1,0:T(8,128)}, f32[648,128]{1,0:T(8,128)S(1)}, u32[]{:S(2)}, u32[]{:S(2)}) collective-permute-start(f32[648,128]{1,0:T(8,128)} %get-tuple-element.57), channel_id=1, source_target_pairs={{0,15},{1,0},{2,1},{3,2},{4,3},{5,4},{6,5},{7,6},{8,7},{9,8},{10,9... | collective-permute-start | bytes 995336 | tf_op jit(solution)/shard_map/ppermute | solution.py:908
  23.1 1.7 %broadcast_in_dim.108 = s32[17,72,2,64]{3,2,1,0:T(2,128)S(1)} broadcast(s32[17,72,2]{2,1,0:T(8,128)S(1)} %pad.40.clone), dimensions={0,1,2} | broadcast | bytes 636480 | tf_op jit(solution)/shard_map/broadcast_in_dim | solution.py:868
  25.5 2.2 %fusion.g3_in = f32[3456,128]{1,0:T(8,128)} fusion(f32[2,128]{1,0:T(2,128)S(1)} %stack.153, f32[3456]{0:T(1024)S(1)} %mul.145, s32[3456]{0:T(1024)S(1)} %ge.72, s32[2,128]{1,0:T(2,128)S(1)} %pad_add_fusion.3), kind=kLoop, calls=%fused_computation.1 | loop fusion | flops 1327104 | bytes 1799168 | tf_op jit(solution)/shard_map/jit(_where)/select_n | solution.py:852
  27.7 1.1 multiply_select_fusion.w_ref
  29.3 0.7 copy-done.12
  30.2 11.4 %shard_map.70 = (f32[3456,128]{1,0:T(8,128)}, f32[3456,128]{1,0:T(8,128)}, f32[432,128]{1,0:T(8,128)}, f32[432,128]{1,0:T(8,128)}, f32[432,128]{1,0:T(8,128)}, /...) custom-call(s32[4]{0:T(128)} %pad_add_fusion.4.ids_ref, ...), custom_call_target="tpu_custom_call" | custom-call | tf_op jit(solution)/shard_map/pallas_call | solution.py:940
  41.6 3.4 %collective-permute-start.7 = (f32[432,128]{1,0:T(8,128)}, f32[432,128]{1,0:T(8,128)S(1)}, u32[]{:S(2)}, u32[]{:S(2)}) collective-permute-start(f32[432,128]{1,0:T(8,128)} %get-tuple-element.67), channel_id=1, source_target_pairs={{0,16},{16,32},{32,48},{48,64},{64,80},{80,96},{96,112},{112,0},{1... | collective-permute-start | bytes 663560 | tf_op jit(solution)/shard_map/ppermute | solution.py:907
  45.0 1.7 %collective-permute-start.4 = (f32[128,128]{1,0:T(8,128)}, f32[128,128]{1,0:T(8,128)S(1)}, u32[]{:S(2)}, u32[]{:S(2)}) collective-permute-start(f32[128,128]{1,0:T(8,128)} %get-tuple-element.60), channel_id=1, source_target_pairs={{0,16},{16,32},{32,48},{48,64},{64,80},{80,96},{96,112},{112,0},{1... | collective-permute-start | bytes 196616 | tf_op jit(solution)/shard_map/ppermute | solution.py:907
  46.9 2.0 %collective-permute-done.4.left_ref = f32[128,128]{1,0:T(8,128)S(1)} collective-permute-done((f32[128,128]{1,0:T(8,128)}, f32[128,128]{1,0:T(8,128)S(1)}, u32[]{:S(2)}, u32[]{:S(2)}) %collective-permute-start.4) | collective-permute-done | bytes 65568 | tf_op jit(solution)/shard_map/ppermute | solution.py:907
  48.9 2.7 %collective-permute-done.5.right_ref = f32[128,128]{1,0:T(8,128)S(1)} collective-permute-done((f32[128,128]{1,0:T(8,128)}, f32[128,128]{1,0:T(8,128)S(1)}, u32[]{:S(2)}, u32[]{:S(2)}) %collective-permute-start.5) | collective-permute-done | bytes 65568 | tf_op jit(solution)/shard_map/ppermute | solution.py:908
  52.2 1.6 %shard_map.71 = (f32[192,128]{1,0:T(8,128)}, f32[192,128]{1,0:T(8,128)}) custom-call(s32[4]{0:T(128)} %pad_add_fusion.4.ids_ref, f32[128,128]{1,0:T(8,128)} %get-tuple-element.62.lo_ref, f32[128,128]{1,0:T(8,128)} %get-tuple-element.63.hi_ref, f32[128,128]{1,0:T(8,128)} %copy-done.14, f32[128,128]{1,0:T(8,128)} %copy-done.15), custom_call_target="tpu_custom_call" | custom-call | tf_op jit(solution)/shard_map/pallas_call | solution.py:950
  53.8 4.8 %collective-permute-start.9 = (f32[192,128]{1,0:T(8,128)}, f32[192,128]{1,0:T(8,128)S(1)}, u32[]{:S(2)}, u32[]{:S(2)}) collective-permute-start(f32[192,128]{1,0:T(8,128)} %get-tuple-element.68), channel_id=1, source_target_pairs={{0,15},{1,0},{2,1},{3,2},{4,3},{5,4},{6,5},{7,6},{8,7},{9,8},{10,9... | collective-permute-start | bytes 294920 | tf_op jit(solution)/shard_map/ppermute | solution.py:908
  59.4 2.1 %shard_map.72 = (f32[648,128]{1,0:T(8,128)}, f32[648,128]{1,0:T(8,128)}) custom-call(s32[4]{0:T(128)} %pad_add_fusion.4.ids_ref, f32[432,128]{1,0:T(8,128)} %get-tuple-element.65.lo_ref, f32[432,128]{1,0:T(8,128)} %get-tuple-element.66.hi_ref, f32[432,128]{1,0:T(8,128)} %copy-done.5, f32[432,128]{1,0:T(8,128)} %copy-done.6), custom_call_target="tpu_custom_call" | custom-call | tf_op jit(solution)/shard_map/pallas_call | solution.py:955
  61.6 4.8 %collective-permute-start.13 = (f32[648,128]{1,0:T(8,128)}, f32[648,128]{1,0:T(8,128)S(1)}, u32[]{:S(2)}, u32[]{:S(2)}) collective-permute-start(f32[648,128]{1,0:T(8,128)} %get-tuple-element.83), channel_id=1, source_target_pairs={{0,15},{1,0},{2,1},{3,2},{4,3},{5,4},{6,5},{7,6},{8,7},{9,8},{10,9... | collective-permute-start | bytes 995336 | tf_op jit(solution)/shard_map/ppermute | solution.py:908
  67.0 5.6 %shard_map.73 = (f32[1024,128]{1,0:T(8,128)}, f32[1024,128]{1,0:T(8,128)}, f32[1024,128]{1,0:T(8,128)}, f32[640,128]{1,0:T(8,128)}, f32[640,128]{1,0:T(8,128)}) custom-call(s32[4]{0:T(128)} %pad_add_fusion.4.ids_ref, f32[1024,128]{1,0:T(8,128)} %get-tuple-element.58.s_ref, f32[1024,128]{1,0:T(8,128)} %get-tuple-element.59.bp_ref, f32[128,128]{1,0:T(8,128)} %copy-done.14, ...), custom_call_target="tpu_custom_call" | custom-call | tf_op jit(solution)/shard_map/pallas_call | solution.py:961
  72.6 1.4 %collective-permute-start.11 = (f32[640,128]{1,0:T(8,128)}, f32[640,128]{1,0:T(8,128)S(1)}, u32[]{:S(2)}, u32[]{:S(2)}) collective-permute-start(f32[640,128]{1,0:T(8,128)} %get-tuple-element.81), channel_id=1, source_target_pairs={{0,16},{16,32},{32,48},{48,64},{64,80},{80,96},{96,112},{112,0},{1... | collective-permute-start | bytes 983048 | tf_op jit(solution)/shard_map/ppermute | solution.py:907
  74.2 4.8 %all-to-all-start = ((f32[64,16,128]{2,1,0:T(8,128)}), f32[64,16,128]{2,1,0:T(8,128)S(1)}, u32[]{:S(2)}, u32[]{:S(2)}) async-start(f32[64,16,128]{2,1,0:T(8,128)} %bitcast.76), calls=%async_computation | async-start | bytes 1048576 | tf_op jit(solution)/shard_map/all_to_all | solution.py:969
  79.1 1.9 %collective-permute-done.14.right_ref.right_in = f32[640,128]{1,0:T(8,128)S(1)} collective-permute-done((f32[640,128]{1,0:T(8,128)}, f32[640,128]{1,0:T(8,128)S(1)}, u32[]{:S(2)}, u32[]{:S(2)}) %collective-permute-start.14) | collective-permute-done | bytes 327712 | tf_op jit(solution)/shard_map/ppermute | solution.py:908
  81.7 2.7 %shard_map.75 = (f32[1472,128]{1,0:T(8,128)}, f32[1472,128]{1,0:T(8,128)}) custom-call(s32[4]{0:T(128)} %pad_add_fusion.4.ids_ref, f32[1024,128]{1,0:T(8,128)} %get-tuple-element.79.r3_ref.r3p_in, f32[1024,128]{1,0:T(8,128)} %get-tuple-element.80.z3_ref.z3p_in, f32[640,128]{1,0:T(8,128)} %copy-done.1, f32[640,128]{1,0:T(8,128)} %copy-done.2), custom_call_target="tpu_custom_call" | custom-call | tf_op jit(solution)/shard_map/pallas_call | solution.py:974
  84.4 4.8 %collective-permute-start.16 = (f32[1472,128]{1,0:T(8,128)}, f32[1472,128]{1,0:T(8,128)S(1)}, u32[]{:S(2)}, u32[]{:S(2)}) collective-permute-start(f32[1472,128]{1,0:T(8,128)} %get-tuple-element.87), channel_id=1, source_target_pairs={{0,15},{1,0},{2,1},{3,2},{4,3},{5,4},{6,5},{7,6},{8,7},{9,8},{10,9... | collective-permute-start | bytes 2261000 | tf_op jit(solution)/shard_map/ppermute | solution.py:908
  89.8 4.5 %collective-permute-start.10 = (f32[1024,128]{1,0:T(8,128)S(1)}, f32[1024,128]{1,0:T(8,128)S(1)}, u32[]{:S(2)}, u32[]{:S(2)}) collective-permute-start(f32[1024,128]{1,0:T(8,128)S(1)} %bitcast.72), channel_id=1, source_target_pairs={{0,16},{16,0},{32,48},{48,32},{64,80},{80,64},{96,112},{112,96},{1... | collective-permute-start | bytes 1572872 | tf_op jit(solution)/shard_map/ppermute | solution.py:971
  94.3 1.5 %collective-permute-done.10.other_ref = f32[1024,128]{1,0:T(8,128)S(1)} collective-permute-done((f32[1024,128]{1,0:T(8,128)S(1)}, f32[1024,128]{1,0:T(8,128)S(1)}, u32[]{:S(2)}, u32[]{:S(2)}) %collective-permute-start.10) | collective-permute-done | bytes 524320 | tf_op jit(solution)/shard_map/ppermute | solution.py:971
  95.9 0.8 copy-done.9
  96.7 12.0 %shard_map.74 = (f32[13,24,128]{2,1,0:T(8,128)}, f32[64,128]{1,0:T(8,128)}) custom-call(s32[4]{0:T(128)} %pad_add_fusion.4.ids_ref, f32[1024,128]{1,0:T(8,128)} %bitcast.73, f32[1024,128]{1,0:T(8,128)} %copy-done.9, f32[17,72,128]{2,1,0:T(8,128)} %multiply_select_fusion.w_ref, bf16[128,128]{1,0:T(8,128)(2,1)} %constant.90.clone.perm_ref), custom_call_target="tpu_custom_call" | custom-call | tf_op jit(solution)/shard_map/pallas_call | solution.py:978
  108.7 0.8 copy-done.7
  109.8 23.8 %shard_map.76 = f32[576,384]{1,0:T(8,128)} custom-call(s32[4]{0:T(128)} %pad_add_fusion.4.ids_ref, f32[13,24,128]{2,1,0:T(8,128)} %get-tuple-element.76.win_ref, f32[3456,128]{1,0:T(8,128)} %get-tuple-element.77.r5p_in, f32[3456,128]{1,0:T(8,128)} %get-tuple-element.78.z5_in, f32[1024,128]{1,0:T(8,128)} %get-tuple-element.79.r3_ref.r3p_in, ...), custom_call_target="tpu_custom_call" | custom-call | tf_op jit(solution)/shard_map/pallas_call | solution.py:988
  (109 shorter events, 9.6 us)
Async XLA Ops:
  0.6 12.1 %copy-start.16 = (s32[32,64]{1,0:T(8,128)S(1)}, s32[32,64]{1,0:T(8,128)}, u32[]{:S(2)}) copy-start(s32[32,64]{1,0:T(8,128)} %param.6) | copy-start | bytes 24580
  5.5 7.3 %collective-permute-start = (f32[432,128]{1,0:T(8,128)}, f32[432,128]{1,0:T(8,128)S(1)}, u32[]{:S(2)}, u32[]{:S(2)}) collective-permute-start(f32[432,128]{1,0:T(8,128)} %get-tuple-element.49), channel_id=1, source_target_pairs={{0,16},{16,32},{32,48},{48,64},{64,80},{80,96},{96,112},{112,0},{1... | collective-permute-start | bytes 663560 | tf_op jit(solution)/shard_map/ppermute | solution.py:907
  8.1 5.6 %collective-permute-start.1 = (f32[432,128]{1,0:T(8,128)}, f32[432,128]{1,0:T(8,128)S(1)}, u32[]{:S(2)}, u32[]{:S(2)}) collective-permute-start(f32[432,128]{1,0:T(8,128)} %get-tuple-element.51), channel_id=1, source_target_pairs={{0,112},{16,0},{32,16},{48,32},{64,48},{80,64},{96,80},{112,96},{1... | collective-permute-start | bytes 663560 | tf_op jit(solution)/shard_map/ppermute | solution.py:908
  12.8 0.9 copy-start.3
  16.5 12.8 %collective-permute-start.2 = (f32[648,128]{1,0:T(8,128)}, f32[648,128]{1,0:T(8,128)S(1)}, u32[]{:S(2)}, u32[]{:S(2)}) collective-permute-start(f32[648,128]{1,0:T(8,128)} %get-tuple-element.54), channel_id=1, source_target_pairs={{0,1},{1,2},{2,3},{3,4},{4,5},{5,6},{6,7},{7,8},{8,9},{9,10},{10,1... | collective-permute-start | bytes 995336 | tf_op jit(solution)/shard_map/ppermute | solution.py:907
  18.1 11.2 %collective-permute-start.3 = (f32[648,128]{1,0:T(8,128)}, f32[648,128]{1,0:T(8,128)S(1)}, u32[]{:S(2)}, u32[]{:S(2)}) collective-permute-start(f32[648,128]{1,0:T(8,128)} %get-tuple-element.57), channel_id=1, source_target_pairs={{0,15},{1,0},{2,1},{3,2},{4,3},{5,4},{6,5},{7,6},{8,7},{9,8},{10,9... | collective-permute-start | bytes 995336 | tf_op jit(solution)/shard_map/ppermute | solution.py:908
  29.3 0.8 copy-start.12
  29.3 0.9 copy-start.13
  41.6 17.0 %collective-permute-start.7 = (f32[432,128]{1,0:T(8,128)}, f32[432,128]{1,0:T(8,128)S(1)}, u32[]{:S(2)}, u32[]{:S(2)}) collective-permute-start(f32[432,128]{1,0:T(8,128)} %get-tuple-element.67), channel_id=1, source_target_pairs={{0,16},{16,32},{32,48},{48,64},{64,80},{80,96},{96,112},{112,0},{1... | collective-permute-start | bytes 663560 | tf_op jit(solution)/shard_map/ppermute | solution.py:907
  45.0 13.6 %collective-permute-start.8 = (f32[432,128]{1,0:T(8,128)}, f32[432,128]{1,0:T(8,128)S(1)}, u32[]{:S(2)}, u32[]{:S(2)}) collective-permute-start(f32[432,128]{1,0:T(8,128)} %get-tuple-element.70), channel_id=1, source_target_pairs={{0,112},{16,0},{32,16},{48,32},{64,48},{80,64},{96,80},{112,96},{1... | collective-permute-start | bytes 663560 | tf_op jit(solution)/shard_map/ppermute | solution.py:908
  45.0 3.9 %collective-permute-start.4 = (f32[128,128]{1,0:T(8,128)}, f32[128,128]{1,0:T(8,128)S(1)}, u32[]{:S(2)}, u32[]{:S(2)}) collective-permute-start(f32[128,128]{1,0:T(8,128)} %get-tuple-element.60), channel_id=1, source_target_pairs={{0,16},{16,32},{32,48},{48,64},{64,80},{80,96},{96,112},{112,0},{1... | collective-permute-start | bytes 196616 | tf_op jit(solution)/shard_map/ppermute | solution.py:907
  46.8 4.8 %collective-permute-start.5 = (f32[128,128]{1,0:T(8,128)}, f32[128,128]{1,0:T(8,128)S(1)}, u32[]{:S(2)}, u32[]{:S(2)}) collective-permute-start(f32[128,128]{1,0:T(8,128)} %get-tuple-element.61), channel_id=1, source_target_pairs={{0,112},{16,0},{32,16},{48,32},{64,48},{80,64},{96,80},{112,96},{1... | collective-permute-start | bytes 196616 | tf_op jit(solution)/shard_map/ppermute | solution.py:908
  48.9 2.7 %copy-start.14 = (f32[128,128]{1,0:T(8,128)}, f32[128,128]{1,0:T(8,128)S(1)}, u32[]{:S(2)}) copy-start(f32[128,128]{1,0:T(8,128)S(1)} %collective-permute-done.4.left_ref) | copy-start | bytes 196612
  53.8 7.7 %collective-permute-start.6 = (f32[192,128]{1,0:T(8,128)}, f32[192,128]{1,0:T(8,128)S(1)}, u32[]{:S(2)}, u32[]{:S(2)}) collective-permute-start(f32[192,128]{1,0:T(8,128)} %get-tuple-element.64), channel_id=1, source_target_pairs={{0,1},{1,2},{2,3},{3,4},{4,5},{5,6},{6,7},{7,8},{8,9},{9,10},{10,1... | collective-permute-start | bytes 294920 | tf_op jit(solution)/shard_map/ppermute | solution.py:907
  53.8 12.6 %collective-permute-start.9 = (f32[192,128]{1,0:T(8,128)}, f32[192,128]{1,0:T(8,128)S(1)}, u32[]{:S(2)}, u32[]{:S(2)}) collective-permute-start(f32[192,128]{1,0:T(8,128)} %get-tuple-element.68), channel_id=1, source_target_pairs={{0,15},{1,0},{2,1},{3,2},{4,3},{5,4},{6,5},{7,6},{8,7},{9,8},{10,9... | collective-permute-start | bytes 294920 | tf_op jit(solution)/shard_map/ppermute | solution.py:908
  58.6 0.8 copy-start.6
  61.5 4.9 %copy-start.17 = (f32[192,128]{1,0:T(8,128)}, f32[192,128]{1,0:T(8,128)S(1)}, u32[]{:S(2)}) copy-start(f32[192,128]{1,0:T(8,128)S(1)} %collective-permute-done.6.low_ref) | copy-start | bytes 294916
  61.5 17.5 %collective-permute-start.12 = (f32[648,128]{1,0:T(8,128)}, f32[648,128]{1,0:T(8,128)S(1)}, u32[]{:S(2)}, u32[]{:S(2)}) collective-permute-start(f32[648,128]{1,0:T(8,128)} %get-tuple-element.82), channel_id=1, source_target_pairs={{0,1},{1,2},{2,3},{3,4},{4,5},{5,6},{6,7},{7,8},{8,9},{9,10},{10,1... | collective-permute-start | bytes 995336 | tf_op jit(solution)/shard_map/ppermute | solution.py:907
  61.6 17.5 %collective-permute-start.13 = (f32[648,128]{1,0:T(8,128)}, f32[648,128]{1,0:T(8,128)S(1)}, u32[]{:S(2)}, u32[]{:S(2)}) collective-permute-start(f32[648,128]{1,0:T(8,128)} %get-tuple-element.83), channel_id=1, source_target_pairs={{0,15},{1,0},{2,1},{3,2},{4,3},{5,4},{6,5},{7,6},{8,7},{9,8},{10,9... | collective-permute-start | bytes 995336 | tf_op jit(solution)/shard_map/ppermute | solution.py:908
  72.6 6.5 %collective-permute-start.11 = (f32[640,128]{1,0:T(8,128)}, f32[640,128]{1,0:T(8,128)S(1)}, u32[]{:S(2)}, u32[]{:S(2)}) collective-permute-start(f32[640,128]{1,0:T(8,128)} %get-tuple-element.81), channel_id=1, source_target_pairs={{0,16},{16,32},{32,48},{48,64},{64,80},{80,96},{96,112},{112,0},{1... | collective-permute-start | bytes 983048 | tf_op jit(solution)/shard_map/ppermute | solution.py:907
  74.0 7.0 %collective-permute-start.14 = (f32[640,128]{1,0:T(8,128)}, f32[640,128]{1,0:T(8,128)S(1)}, u32[]{:S(2)}, u32[]{:S(2)}) collective-permute-start(f32[640,128]{1,0:T(8,128)} %get-tuple-element.85), channel_id=1, source_target_pairs={{0,112},{16,0},{32,16},{48,32},{64,48},{80,64},{96,80},{112,96},{1... | collective-permute-start | bytes 983048 | tf_op jit(solution)/shard_map/ppermute | solution.py:908
  74.2 15.6 %all-to-all-start = ((f32[64,16,128]{2,1,0:T(8,128)}), f32[64,16,128]{2,1,0:T(8,128)S(1)}, u32[]{:S(2)}, u32[]{:S(2)}) async-start(f32[64,16,128]{2,1,0:T(8,128)} %bitcast.76), calls=%async_computation | async-start | bytes 1048576 | tf_op jit(solution)/shard_map/all_to_all | solution.py:969
  79.0 2.0 %copy-start.1 = (f32[640,128]{1,0:T(8,128)}, f32[640,128]{1,0:T(8,128)S(1)}, u32[]{:S(2)}) copy-start(f32[640,128]{1,0:T(8,128)S(1)} %collective-permute-done.11.left_ref.left_in) | copy-start | bytes 983044
  79.0 29.6 %copy-start.10 = (f32[648,128]{1,0:T(8,128)}, f32[648,128]{1,0:T(8,128)S(1)}, u32[]{:S(2)}) copy-start(f32[648,128]{1,0:T(8,128)S(1)} %collective-permute-done.12.low5_in) | copy-start | bytes 995332
  79.1 29.6 %copy-start.11 = (f32[648,128]{1,0:T(8,128)}, f32[648,128]{1,0:T(8,128)S(1)}, u32[]{:S(2)}) copy-start(f32[648,128]{1,0:T(8,128)S(1)} %collective-permute-done.13.high5_in) | copy-start | bytes 995332
  84.4 24.2 %collective-permute-start.15 = (f32[1472,128]{1,0:T(8,128)}, f32[1472,128]{1,0:T(8,128)S(1)}, u32[]{:S(2)}, u32[]{:S(2)}) collective-permute-start(f32[1472,128]{1,0:T(8,128)} %get-tuple-element.86), channel_id=1, source_target_pairs={{0,1},{1,2},{2,3},{3,4},{4,5},{5,6},{6,7},{7,8},{8,9},{9,10},{10,1... | collective-permute-start | bytes 2261000 | tf_op jit(solution)/shard_map/ppermute | solution.py:907
  84.4 24.2 %collective-permute-start.16 = (f32[1472,128]{1,0:T(8,128)}, f32[1472,128]{1,0:T(8,128)S(1)}, u32[]{:S(2)}, u32[]{:S(2)}) collective-permute-start(f32[1472,128]{1,0:T(8,128)} %get-tuple-element.87), channel_id=1, source_target_pairs={{0,15},{1,0},{2,1},{3,2},{4,3},{5,4},{6,5},{7,6},{8,7},{9,8},{10,9... | collective-permute-start | bytes 2261000 | tf_op jit(solution)/shard_map/ppermute | solution.py:908
  89.8 6.1 %copy-start = (f32[64,16,128]{2,1,0:T(8,128)}, f32[64,16,128]{2,1,0:T(8,128)S(1)}, u32[]{:S(2)}) copy-start(f32[64,16,128]{2,1,0:T(8,128)S(1)} %all-to-all-done) | copy-start | bytes 1572868
  89.8 6.1 %collective-permute-start.10 = (f32[1024,128]{1,0:T(8,128)S(1)}, f32[1024,128]{1,0:T(8,128)S(1)}, u32[]{:S(2)}, u32[]{:S(2)}) collective-permute-start(f32[1024,128]{1,0:T(8,128)S(1)} %bitcast.72), channel_id=1, source_target_pairs={{0,16},{16,0},{32,48},{48,32},{64,80},{80,64},{96,112},{112,96},{1... | collective-permute-start | bytes 1572872 | tf_op jit(solution)/shard_map/ppermute | solution.py:971
  95.9 0.8 copy-start.9
  108.6 0.9 copy-start.7
  108.7 1.1 copy-start.8
  (5 other events, 3.3 us)
